TPU v7x, 128 devices: a whole 4x4x4 slice. The times are simulated.
128 devices in a mesh: ctx: 64 (over x, y, z), head: 2 (over core).
Axes of the slice: x: 4, y: 4, z: 4, core: 2. Of those that a mesh axis runs over, the one named last changes fastest.
Arguments:
- queries: bfloat16 [32768, 32, 128], P(('ctx', 'head')), may hold values from -112 to 112
- key_states: bfloat16 [32768, 8, 128], P(('ctx', 'head')), may hold values from -4 to 4
- value_states: bfloat16 [32768, 8, 128], P(('ctx', 'head')), may hold values from -5 to 5
- column_blocks: int32 [32, 4], replicated, may hold values from 0 to 255, as said below
- column_count: int32 [32], replicated, may hold values from 1 to 4
- slash_offsets: int32 [32, 16], replicated, may hold values from 0 to 255, as said below
- slash_count: int32 [32], replicated, may hold values from 1 to 16
Outputs:
- attended: bfloat16 [32768, 32, 128], P(('ctx', 'head'))
Inputs may be any that keep to these rules, and one draw needn't show every extreme that they name: `column_blocks`: the 4 entries of a head's row are distinct block numbers. `slash_offsets`: the entries of a head's row are distinct and the first is 0.
All inputs are finite; a program needn't handle non-finite values.
Results may differ from a plain program's by a relative error of at most 0.003.
Values may be sent and summed in bfloat16 or wider, within the bound.
A program may use at most 128 MiB of HBM per device.

v0:
```python
import math

import jax
import jax.numpy as jnp
from jax import lax
from jax.sharding import PartitionSpec as P

BLOCK = 128
SSLOTS = 16
BAND = 256


def passed_along(block, axis, distance):
    devices = range(lax.axis_size(axis))
    route = [(i - distance, i) for i in devices if i - distance in devices]
    return lax.ppermute(block, axis, route)


def body(
    queries, key_states, value_states, column_blocks, column_count, slash_offsets, slash_count
):
    query_local, key_local, value_local = (
        lax.all_to_all(queries, "head", split_axis=1, concat_axis=0, tiled=True),
        lax.all_to_all(key_states, "head", split_axis=1, concat_axis=0, tiled=True),
        lax.all_to_all(value_states, "head", split_axis=1, concat_axis=0, tiled=True),
    )
    token_count = query_local.shape[0]
    head_count = query_local.shape[1]
    kv_heads_here = key_local.shape[1]
    per_group = head_count // kv_heads_here
    head_depth = query_local.shape[2]
    slot_total = column_blocks.shape[1]
    ctx_rank = lax.axis_index("ctx")
    head_rank = lax.axis_index("head")
    head_first = head_rank * head_count
    my_blocks = lax.dynamic_slice_in_dim(column_blocks, head_first, head_count, 0)
    my_vcount = lax.dynamic_slice_in_dim(column_count, head_first, head_count, 0)
    my_offsets = lax.dynamic_slice_in_dim(slash_offsets, head_first, head_count, 0)
    my_scount = lax.dynamic_slice_in_dim(slash_count, head_first, head_count, 0)
    slot_live = jnp.arange(slot_total, dtype=jnp.int32)[None, :] < my_vcount[:, None]
    offset_live = jnp.arange(SSLOTS, dtype=jnp.int32)[None, :] < my_scount[:, None]
    start_token = ctx_rank * token_count
    column_pos = (
        my_blocks[:, :, None] * BLOCK + jnp.arange(BLOCK, dtype=jnp.int32)[None, None, :]
    ).reshape(head_count, slot_total * BLOCK)
    column_live = jnp.repeat(slot_live, BLOCK, axis=1)
    local_rows = column_pos - start_token
    owned = (local_rows >= 0) & (local_rows < token_count)
    safe_rows = jnp.clip(local_rows, 0, token_count - 1)
    owner_head = jnp.arange(head_count, dtype=jnp.int32) // per_group
    pairs_local = jnp.concatenate([key_local, value_local], axis=2)
    picked = pairs_local[safe_rows, owner_head[:, None]]
    payload = jnp.where(owned[:, :, None], picked.astype(jnp.float32), 0.0)
    columns = lax.psum(payload, "ctx").astype(jnp.bfloat16)
    tail_rows = pairs_local[token_count - BAND :]
    before_rows = passed_along(tail_rows, "ctx", 1)
    window_all = jnp.concatenate([before_rows, pairs_local], axis=0)
    rows_block = min(512, token_count)
    scale_factor = 1.0 / math.sqrt(head_depth)
    query_pos = start_token + 0 + jnp.arange(rows_block, dtype=jnp.int32)
    window_pos = start_token + 0 - BAND + jnp.arange(BAND + rows_block, dtype=jnp.int32)
    gap_rows = query_pos[:, None] - window_pos[None, :]
    pieces = []
    for kv_head in range(kv_heads_here):
        head_low = kv_head * per_group
        head_high = head_low + per_group
        query_rows = query_local[0:rows_block, head_low:head_high]
        window_rows = window_all[0 : BAND + rows_block, kv_head]
        group_columns = columns[head_low:head_high]
        band_scores = (
            jnp.einsum(
                "qhd,kd->hqk",
                query_rows,
                window_rows[:, :head_depth],
                preferred_element_type=jnp.float32,
            )
            * scale_factor
        )
        column_scores = (
            jnp.einsum(
                "qhd,hkd->hqk",
                query_rows,
                group_columns[:, :, :head_depth],
                preferred_element_type=jnp.float32,
            )
            * scale_factor
        )
        group_offsets = my_offsets[head_low:head_high]
        group_olive = offset_live[head_low:head_high]
        on_slash = jnp.zeros((per_group, rows_block, BAND + rows_block), jnp.bool_)
        for slot_index in range(SSLOTS):
            on_slash = (
                on_slash
                | (gap_rows[None] == group_offsets[:, slot_index][:, None, None])
                & group_olive[:, slot_index][:, None, None]
            )
        in_columns = jnp.any(
            ((window_pos // BLOCK)[None, :, None] == my_blocks[head_low:head_high][:, None, :])
            & slot_live[head_low:head_high][:, None, :],
            axis=2,
        )
        band_ok = (
            on_slash
            & (gap_rows >= 0)[None]
            & (window_pos >= 0)[None, None, :]
            & jnp.logical_not(in_columns)[:, None, :]
        )
        column_ok = column_live[head_low:head_high][:, None, :] & (
            column_pos[head_low:head_high][:, None, :] <= query_pos[None, :, None]
        )
        band_top = jnp.max(jnp.where(band_ok, band_scores, -jnp.inf), axis=2, keepdims=True)
        column_top = jnp.max(jnp.where(column_ok, column_scores, -jnp.inf), axis=2, keepdims=True)
        row_top = jnp.maximum(band_top, column_top)
        band_weights = jnp.where(band_ok, jnp.exp(band_scores - row_top), 0.0)
        column_weights = jnp.where(column_ok, jnp.exp(column_scores - row_top), 0.0)
        row_total = jnp.sum(band_weights, axis=2) + jnp.sum(column_weights, axis=2)
        mixed = jnp.einsum(
            "hqk,kd->qhd",
            band_weights.astype(jnp.bfloat16),
            window_rows[:, head_depth:],
            preferred_element_type=jnp.float32,
        )
        mixed = mixed + jnp.einsum(
            "hqk,hkd->qhd",
            column_weights.astype(jnp.bfloat16),
            group_columns[:, :, head_depth:],
            preferred_element_type=jnp.float32,
        )
        pieces.append((mixed / row_total.T[:, :, None]).astype(jnp.bfloat16))
    outputs = jnp.concatenate(pieces, axis=1)
    return lax.all_to_all(outputs, "head", split_axis=0, concat_axis=1, tiled=True)


def solution(mesh):
    placed = (
        P(("ctx", "head"), None, None),
        P(("ctx", "head"), None, None),
        P(("ctx", "head"), None, None),
        P(),
        P(),
        P(),
        P(),
    )
    return jax.shard_map(
        body, mesh=mesh, in_specs=placed, out_specs=P(("ctx", "head"), None, None), check_vma=False
    )
```

profile of v0, /device:TPU:1, one launch (start us, length us, event | category | flops | bytes accessed | tf_op | source)
XLA Modules:
  0.0 685.8 jit_solution(6624796421530442441)
XLA Ops:
  0.0 2.0 copy.64
  2.0 4.9 all-to-all-start
  6.9 0.9 copy.66
  7.7 0.5 all-to-all-done
  8.2 4.6 all-to-all-start.1
  12.8 1.5 all-to-all-done.1
  14.3 1.1 copy.67
  15.4 0.9 fusion.104
  16.3 4.4 collective-permute-start
  20.7 2.1 copy.69
  22.8 4.5 all-to-all-start.2
  27.5 0.6 slice_bitcast_fusion.71
  28.1 1.3 broadcast_subtract_fusion
  29.5 1.1 broadcast_compare_fusion
  30.6 1.1 pad_maximum_fusion.1
  31.7 1.5 copy.70
  33.2 0.1 copy.71
  33.3 0.1 iota_add_fusion
  33.6 2.0 copy.72
  35.6 81.5 %gather_fusion = bf16[8192,256]{1,0:T(8,128)(2,1)} fusion(bf16[512,4,256]{2,1,0:T(4,128)(2,1)S(1)} %copy.72, s32[8192]{0:T(1024)S(1)} %bitcast.547), kind=kCustom, calls=%fused_computation | custom fusion | bytes 8454144 | tf_op jit(solution)/shard_map/gather | solution.py:52
  117.1 6.8 convert_select_fusion
  123.9 364.1 %all-reduce.1 = bf16[16,512,256]{2,1,0:T(8,128)(2,1)} all-reduce(f32[16,512,256]{2,1,0:T(8,128)} %convert_select_fusion), channel_id=1, replica_groups=mesh['ctx'=64,'head'=2] {'ctx'}, use_global_device_ids=true, to_apply=%region_2.3 | all-reduce | flops 2097152 | bytes 12582912 | tf_op jit(solution)/shard_map/psum | solution.py:54
  488.0 3.7 fusion.106
  491.7 3.8 fusion.109
  495.5 0.7 slice_bitcast_fusion.54
  496.2 0.7 slice_bitcast_fusion.55
  496.9 0.1 copy.68
  497.0 0.1 copy.77
  497.1 0.1 copy.82
  497.2 0.1 copy.87
  497.5 0.1 broadcast_bitcast_fusion.2
  497.6 0.1 broadcast_bitcast_fusion
  497.6 0.2 and_reduce_fusion.3
  497.9 0.8 fusion.141
  498.7 0.6 fusion.136
  499.4 0.2 fusion.140
  499.5 3.4 fusion.21
  502.9 1.2 maximum_maximum_fusion
  504.4 0.1 slice_bitcast_fusion.1
  504.6 1.2 copy-done.6
  505.7 0.3 copy-done.18
  506.3 28.6 %fusion.9 = (f32[4,512]{1,0:T(4,128)S(1)}, pred[4,512,768]{1,2,0:T(32,128)(4,1)}, f32[768,512,4]{1,0,2:T(8,128)S(1)}) fusion(pred[4,768]{1,0:T(4,128)(4,1)S(1)} %not.28, pred[768]{0:T(1024)(128)(4,1)S(1)} %copy-done.65, pred[512,768]{0,1:T(8,128)(4,1)S(1)} %copy-done.18, pred[4]{0:T(512)(128)(4,1)S(1)} %copy-done.22, s32[4]{0:T(128)S(1)} %copy-done.48, ...), kind=kOutput, calls=%fused_computation.19 | convolution fusion | flops 486012928 | bytes 10579968 | tf_op jit(solution)/shard_map/qhd,kd->hqk/dot_general | solution.py:71
  534.9 3.0 fusion.60
  537.9 0.8 copy-done.1
  538.9 6.2 fusion.40
  545.2 16.7 %fusion.3 = (f32[4,512]{1,0:T(4,128)S(1)}, pred[4,512,768]{1,2,0:T(32,128)(4,1)}, f32[768,512,4]{1,0,2:T(8,128)S(1)}) fusion(pred[4,768]{1,0:T(4,128)(4,1)S(1)} %not.30, pred[768]{0:T(1024)(128)(4,1)S(1)} %copy-done.65, pred[512,768]{0,1:T(8,128)(4,1)S(1)} %copy-done.18, pred[4]{0:T(512)(128)(4,1)S(1)} %copy-done.45, s32[4]{0:T(128)S(1)} %get-tuple-element.50, ...), kind=kOutput, calls=%fused_computation.9 | convolution fusion | flops 486012928 | bytes 10579968 | tf_op jit(solution)/shard_map/qhd,kd->hqk/dot_general | solution.py:71
  561.9 3.0 fusion.66
  564.9 16.5 %fusion.6 = (f32[4,512]{1,0:T(4,128)S(1)}, pred[4,512,768]{1,2,0:T(32,128)(4,1)}, f32[768,512,4]{1,0,2:T(8,128)S(1)}) fusion(pred[4,768]{1,0:T(4,128)(4,1)S(1)} %not.29, pred[768]{0:T(1024)(128)(4,1)S(1)} %copy-done.65, pred[512,768]{0,1:T(8,128)(4,1)S(1)} %copy-done.18, pred[4]{0:T(512)(128)(4,1)S(1)} %get-tuple-element.130, s32[4]{0:T(128)S(1)} %get-tuple-element.65, ...), kind=kOutput, calls=%fused_computation.14 | convolution fusion | flops 486012928 | bytes 10579968 | tf_op jit(solution)/shard_map/qhd,kd->hqk/dot_general | solution.py:71
  581.4 18.2 %fusion = (f32[4,512]{1,0:T(4,128)S(1)}, pred[4,512,768]{1,2,0:T(32,128)(4,1)}, f32[768,512,4]{1,0,2:T(8,128)S(1)}) fusion(pred[4,768]{1,0:T(4,128)(4,1)S(1)} %not.31, pred[768]{0:T(1024)(128)(4,1)S(1)} %copy-done.66, pred[512,768]{0,1:T(8,128)(4,1)} %broadcast_compare_fusion, pred[4]{0:T(512)(128)(4,1)S(1)} %get-tuple-element.99, ...), kind=kOutput, calls=%fused_computation.4 | convolution fusion | flops 486012928 | bytes 10579968 | tf_op jit(solution)/shard_map/qhd,kd->hqk/dot_general | solution.py:71
  599.6 4.4 fusion.63
  604.1 4.5 fusion.42
  608.6 3.2 fusion.69
  611.8 1.6 fusion.24
  613.5 1.7 divide_convert_fusion.3
  615.3 1.7 fusion.26
  617.0 1.7 divide_convert_fusion.2
  618.7 1.7 fusion.28
  620.4 1.8 divide_convert_fusion.1
  622.2 1.6 fusion.30
  623.9 2.2 divide_convert_fusion
  626.1 0.3 pad_maximum_fusion
  626.3 3.1 copy.92
  629.4 54.6 %all_to_all.72 = bf16[512,16,128]{2,1,0:T(8,128)(2,1)S(1)} all-to-all(bf16[512,16,128]{2,1,0:T(8,128)(2,1)} %copy.92), channel_id=1, replica_groups=mesh['ctx'=64,'head'=2] {'head'}, dimensions={0} | all-to-all | bytes 4194304 | tf_op jit(solution)/shard_map/all_to_all | solution.py:131
  684.0 1.7 copy.93
  (179 shorter events, 1.1 us)
Async XLA Ops:
  0.0 6.9 %copy-start.11 = (bf16[256,8,128]{2,1,0:T(8,128)(2,1)S(1)}, bf16[256,8,128]{2,1,0:T(8,128)(2,1)}, u32[]{:S(2)}) copy-start(bf16[256,8,128]{2,1,0:T(8,128)(2,1)} %param.9) | copy-start | bytes 1572868
  2.0 6.3 all-to-all-start
  8.2 6.1 all-to-all-start.1
  12.8 7.9 %copy-start.5 = (bf16[256,32,128]{2,1,0:T(8,128)(2,1)S(1)}, bf16[256,32,128]{2,1,0:T(8,128)(2,1)}, u32[]{:S(2)}) copy-start(bf16[256,32,128]{2,1,0:T(8,128)(2,1)} %param.7) | copy-start | bytes 6291460
  16.3 486.7 %collective-permute-start = (bf16[256,4,256]{2,0,1:T(8,128)(2,1)}, bf16[256,4,256]{2,0,1:T(8,128)(2,1)}, u32[]{:S(2)}, u32[]{:S(2)}) collective-permute-start(bf16[256,4,256]{2,0,1:T(8,128)(2,1)} %fusion.104), channel_id=1, source_target_pairs={{0,2},{2,4},{4,6},{6,8},{8,10},{10,12},{12,14},{14,16},{16,18},{18... | collective-permute-start | bytes 1572872 | tf_op jit(solution)/shard_map/ppermute | solution.py:16
  22.8 4.5 copy-start.63
  22.8 8.9 %all-to-all-start.2 = ((bf16[256,32,128]{2,0,1:T(8,128)(2,1)}), bf16[256,32,128]{2,0,1:T(8,128)(2,1)S(1)}, u32[]{:S(2)}, u32[]{:S(2)}) async-start(bf16[256,32,128]{2,0,1:T(8,128)(2,1)} %copy.69), calls=%async_computation.2 | async-start | bytes 4194304 | tf_op jit(solution)/shard_map/all_to_all | solution.py:23
  27.4 4.3 copy-start.20
  123.9 364.1 %copy-start.3 = (bf16[256,2,16,128]{3,0,1,2:T(8,128)(2,1)S(1)}, bf16[256,2,16,128]{3,0,1,2:T(8,128)(2,1)}, u32[]{:S(2)}) copy-start(bf16[256,2,16,128]{3,0,1,2:T(8,128)(2,1)} %copy.70) | copy-start | bytes 6291460
  491.7 5.6 copy-start.64
  491.7 6.2 copy-start.19
  504.2 1.9 copy-start.18
  504.2 1.9 copy-start.22
  504.2 1.9 copy-start.23
  504.2 1.9 copy-start.24
  504.2 1.9 copy-start.25
  504.2 1.9 copy-start.26
  504.2 1.9 copy-start.27
  504.2 1.9 copy-start.28
  504.2 1.9 copy-start.29
  504.2 1.9 copy-start.30
  504.3 1.9 copy-start.47
  504.3 1.9 copy-start.48
  504.3 1.9 copy-start.49
  504.3 1.9 copy-start.50
  504.3 1.9 copy-start.51
  504.3 1.9 copy-start.52
  504.3 1.9 copy-start.53
  504.3 1.9 copy-start.54
  504.3 1.9 copy-start.55
  504.3 1.9 copy-start.56
  504.4 1.9 copy-start.57
  504.4 1.9 copy-start.58
  504.4 1.9 copy-start.59
  504.4 1.9 copy-start.60
  504.4 1.9 copy-start.61
  504.4 1.9 copy-start.62
  504.4 1.9 copy-start.65
  504.5 30.4 %copy-start.16 = (bf16[768,256]{1,0:T(8,128)(2,1)}, bf16[768,256]{1,0:T(8,128)(2,1)S(1)}, u32[]{:S(2)}) copy-start(bf16[768,256]{1,0:T(8,128)(2,1)S(1)} %get-tuple-element.29) | copy-start | bytes 1179652
  504.5 40.5 %copy-start.12 = (bf16[768,256]{1,0:T(8,128)(2,1)}, bf16[768,256]{1,0:T(8,128)(2,1)S(1)}, u32[]{:S(2)}) copy-start(bf16[768,256]{1,0:T(8,128)(2,1)S(1)} %get-tuple-element.26) | copy-start | bytes 1179652
  504.6 60.3 %copy-start.14 = (bf16[768,256]{1,0:T(8,128)(2,1)}, bf16[768,256]{1,0:T(8,128)(2,1)S(1)}, u32[]{:S(2)}) copy-start(bf16[768,256]{1,0:T(8,128)(2,1)S(1)} %get-tuple-element.28) | copy-start | bytes 1179652
  506.3 28.6 %copy-start.2 = (bf16[16,512,256]{2,1,0:T(8,128)(2,1)S(1)}, bf16[16,512,256]{2,1,0:T(8,128)(2,1)}, u32[]{:S(2)}) copy-start(bf16[16,512,256]{2,1,0:T(8,128)(2,1)} %all-reduce.1) | copy-start | bytes 12582916
  534.9 3.0 copy-start
  534.9 3.8 copy-start.1
  538.8 6.3 copy-start.31
  538.8 6.3 copy-start.32
  538.8 6.3 copy-start.33
  538.8 6.3 copy-start.34
  538.8 6.3 copy-start.35
  538.8 6.3 copy-start.36
  538.8 6.3 copy-start.37
  538.8 6.3 copy-start.38
  538.8 6.3 copy-start.39
  538.8 6.3 copy-start.40
  538.8 6.3 copy-start.41
  538.8 6.3 copy-start.42
  538.9 6.3 copy-start.43
  538.9 6.3 copy-start.44
  538.9 6.3 copy-start.45
  538.9 6.3 copy-start.46
  561.9 3.0 copy-start.21
  564.9 16.5 %copy-start.66 = (pred[768]{0:T(1024)(128)(4,1)S(1)}, pred[768]{0:T(1024)(128)(4,1)}, u32[]{:S(2)}) copy-start(pred[768]{0:T(1024)(128)(4,1)} %fusion.136) | copy-start | bytes 2308
  599.6 4.4 copy-start.4
  608.6 3.2 copy-start.7
  (11 other events, 18.6 us)
where the time goes:
time: 692 us; the launch traced here: 686 us
  blocking collectives  419 us (61%)
  matrix products  118 us (17%)
  local copies, waits for them, and re-layouts  102 us (15%)
  other arithmetic  25 us (4%)
  starting transfers between devices  18.4 us (3%)
    psum x1, blocking collectives, body(): columns = lax.psum(payload, 'ctx').astype(jnp.bfloat16)  364 us
    gather x1, local copies, waits for them, and re-layouts, body(): picked = pairs_local[safe_rows, owner_head[:, None]]  81.5 us
    dot_general x4, matrix products, body(): jnp.einsum('qhd,kd->hqk', query_rows, window_rows[:, :head_depth], prefer...  80 us
    all_to_all x1, blocking collectives, body(): lax.all_to_all(outputs, 'head', split_axis=0, concat_axis=1, tiled=True)  54.6 us
    dot_general x4, matrix products, body(): jnp.einsum('qhd,hkd->hqk', query_rows, group_columns[:, :, :head_depth],...  17.1 us
  transfers between devices with their start and end apart: 4, of which 2 were waited for; matrix products, arithmetic and copies ran while one was open for 17% of the time, Pallas kernels for 0%

commit v1 on v0

v1 whole, which is shorter than its diff:
```python
import functools
import math

import jax
import jax.numpy as jnp
from jax import lax
from jax.experimental import pallas as pl
from jax.experimental.pallas import tpu as pltpu
from jax.sharding import PartitionSpec as P

HEADS = 32
KV_HEADS = 8
HDIM = 128
BLOCK = 128
VSLOTS = 4
SSLOTS = 16
BAND = 256
CTX = 64
SIDE = 4
NEG = -1e30
MESH = pl.DeviceIdType.MESH
BF16 = jnp.bfloat16


def gather_kernel(
    Q, R, sel_ref, own_ref, kv_ref, g_ref, halo_ref, send, recv, home,
    s1_send, s1_recv, st_send, st_recv, sib_send, sib_recv, loc_sem, halo_send, halo_recv,
):
    c = lax.axis_index("ctx")
    k = lax.axis_index("head")
    coords = (c // 16, (c // 4) % 4, c % 4)
    x, y, z = coords
    barrier = pltpu.get_barrier_semaphore()

    @pl.loop(1, CTX)
    def _(d):
        pl.semaphore_signal(barrier, inc=1, device_id={"ctx": (c + d) % CTX}, device_id_type=MESH)

    pl.semaphore_signal(barrier, inc=1, device_id={"head": 1 - k}, device_id_type=MESH)

    @pl.when(k == 0)
    def _():
        pl.semaphore_signal(
            barrier, inc=1, device_id={"ctx": (c + CTX - 1) % CTX, "head": 1}, device_id_type=MESH
        )

    for r in range(R):
        for u in range(8):
            send[r, u] = kv_ref[sel_ref[r * 8 + u]]
    pl.semaphore_wait(barrier, CTX + k)

    @pl.loop(1, CTX)
    def _(d):
        p = (c + d) % CTX
        for r in range(R):
            pltpu.make_async_remote_copy(
                src_ref=send.at[r, p // 8, pl.ds((p % 8) * 16, 16)],
                dst_ref=recv.at[r, c],
                send_sem=s1_send,
                recv_sem=s1_recv,
                device_id={"ctx": p},
                device_id_type=MESH,
            ).start()

    halo = pltpu.make_async_remote_copy(
        src_ref=kv_ref,
        dst_ref=halo_ref,
        send_sem=halo_send,
        recv_sem=halo_recv,
        device_id={"ctx": (c + k) % CTX, "head": 1 - k},
        device_id_type=MESH,
    )
    halo.start()
    for r in range(R):
        recv[r, c] = send[r, c // 8, pl.ds((c % 8) * 16, 16)]
    others = recv.at[:, pl.ds(0, CTX - 1)]
    pltpu.make_async_copy(others, others, s1_recv).wait()
    for q in range(Q):
        home[q] = recv[q % R, own_ref[q]]
    own_copy = pltpu.make_async_copy(home, g_ref.at[k, :, x, y, z], loc_sem)
    own_copy.start()
    own_copy.wait()

    def along(axis, delta):
        there = list(coords)
        there[axis] = (there[axis] + delta) % SIDE
        return {"ctx": there[0] * 16 + there[1] * 4 + there[2]}

    bounds = [0, (Q + 2) // 3, (2 * Q + 2) // 3, Q]

    def view(t, s, pos, half=None):
        index = [None] * 3
        for i in range(3):
            axis = (t + i) % 3
            index[axis] = slice(None) if i < s else pos if i == s else coords[axis]
        lanes = slice(None) if half is None else pl.ds(half * 128, 128)
        rows = pl.ds(bounds[t], bounds[t + 1] - bounds[t])
        return g_ref.at[k, rows, index[0], index[1], index[2], :, lanes]

    def push(ref, t, s, i, device):
        copy = pltpu.make_async_remote_copy(
            src_ref=ref, dst_ref=ref, send_sem=st_send.at[t, s, i], recv_sem=st_recv.at[t, s, i],
            device_id=device, device_id_type=MESH,
        )
        copy.start()
        return copy

    pending = []
    across = []

    def to_sibling(ref):
        i = len(across)
        copy = pltpu.make_async_remote_copy(
            src_ref=ref, dst_ref=ref, send_sem=sib_send.at[i], recv_sem=sib_recv.at[i],
            device_id={"head": 1 - k}, device_id_type=MESH,
        )
        copy.start()
        across.append(copy)

    first = {}

    def begin(t, s):
        axis = (t + s) % 3
        own = view(t, s, coords[axis])
        first[t] = (push(own, t, s, 0, along(axis, 1)), push(own, t, s, 1, along(axis, -1)))

    def middle(t, s):
        axis = (t + s) % 3
        me = coords[axis]
        left, right = (me + 3) % 4, (me + 1) % 4
        to_right, to_left = first[t]
        to_right.wait_recv()
        on_right = push(view(t, s, left, 0), t, s, 2, along(axis, 1))
        to_left.wait_recv()
        on_left = push(view(t, s, right, 1), t, s, 3, along(axis, -1))
        if s == 2:
            to_sibling(view(t, s, left))
            to_sibling(view(t, s, right))
        pending.extend([to_right, to_left, on_right, on_left])
        return on_right, on_left

    def end(t, s, on_right, on_left):
        axis = (t + s) % 3
        on_right.wait_recv()
        on_left.wait_recv()
        if s == 2:
            to_sibling(view(t, s, (coords[axis] + 2) % 4))

    for t in range(3):
        begin(t, 0)
    for s in range(3):
        passed = [middle(t, s) for t in range(3)]
        for t in range(3):
            end(t, s, *passed[t])
            if s < 2:
                begin(t, s + 1)
            if s == 1:
                to_sibling(view(t, 2, coords[(t + 2) % 3]))
    halo.wait_recv()
    for copy in across:
        copy.wait_recv()
    for copy in pending:
        copy.wait_send()
    for copy in across:
        copy.wait_send()
    halo.wait_send()
    pltpu.make_async_copy(others, others, s1_send).wait()


def gather_pairs(sel, own, kv, Q, R, collective_id):
    return pl.pallas_call(
        functools.partial(gather_kernel, Q, R),
        out_shape=(
            jax.ShapeDtypeStruct((2, Q, 4, 4, 4, 16, 256), BF16),
            jax.ShapeDtypeStruct((16, 128, 256), BF16),
        ),
        in_specs=[
            pl.BlockSpec(memory_space=pltpu.SMEM),
            pl.BlockSpec(memory_space=pltpu.SMEM),
            pl.BlockSpec(memory_space=pltpu.VMEM),
        ],
        out_specs=(pl.BlockSpec(memory_space=pl.ANY), pl.BlockSpec(memory_space=pl.ANY)),
        scratch_shapes=[
            pltpu.VMEM((R, 8, 128, 256), BF16),
            pltpu.VMEM((R, CTX, 16, 256), BF16),
            pltpu.VMEM((Q, 16, 256), BF16),
            pltpu.SemaphoreType.DMA(()),
            pltpu.SemaphoreType.DMA(()),
            pltpu.SemaphoreType.DMA((3, 3, 4)),
            pltpu.SemaphoreType.DMA((3, 3, 4)),
            pltpu.SemaphoreType.DMA((12,)),
            pltpu.SemaphoreType.DMA((12,)),
            pltpu.SemaphoreType.DMA(()),
            pltpu.SemaphoreType.DMA(()),
            pltpu.SemaphoreType.DMA(()),
        ],
        compiler_params=pltpu.CompilerParams(
            collective_id=collective_id, has_side_effects=True, vmem_limit_bytes=32 * 2**20
        ),
    )(sel, own, kv)


LOG2E = 1.4426950408889634
GROUPS = 2


def attend_kernel(
    slot_ref, code_ref, q_ref, kv_ref, halo_ref, base_ref, cbias_ref, g_ref, o_ref, cols, sems
):
    step = pl.program_id(0)
    steps = pl.num_programs(0)
    per_step = GROUPS * 4 * VSLOTS

    def fetch(at, slot):
        for i in range(per_step):
            pltpu.make_async_copy(
                g_ref.at[slot_ref[at * per_step + i]],
                cols.at[slot, i // VSLOTS, pl.ds((i % VSLOTS) * BLOCK, BLOCK)],
                sems.at[slot],
            ).start()

    @pl.when(step == 0)
    def _():
        fetch(0, 0)

    @pl.when(step + 1 < steps)
    def _():
        fetch(step + 1, (step + 1) % 2)

    now = step % 2
    q8 = jnp.swapaxes(q_ref[...], 0, 1)
    row = lax.broadcasted_iota(jnp.int32, (BLOCK, BLOCK), 0)
    col = lax.broadcasted_iota(jnp.int32, (BLOCK, BLOCK), 1)
    triangle = jnp.where(col <= row, 0.0, NEG)
    factor = LOG2E / math.sqrt(HDIM)
    nt = (((1,), (1,)), ((), ()))
    pltpu.make_async_copy(cols.at[now], cols.at[now], sems.at[now]).wait()
    outs = [[None, None] for _ in range(GROUPS * 4)]
    for group in range(GROUPS):
        window = jnp.concatenate([halo_ref[group], kv_ref[group]], axis=0)
        tables = []
        for hh in range(4):
            line = base_ref[pl.ds(group * 4 + hh, 1), :]
            tables.append(
                pltpu.roll(
                    jnp.broadcast_to(line, (BLOCK, 3 * BLOCK)), 0, 1, stride=1, stride_axis=0
                )
            )
        for j in range(2):
            keys = window[j * BLOCK : j * BLOCK + 3 * BLOCK, :HDIM]
            values = window[j * BLOCK : j * BLOCK + 3 * BLOCK, HDIM:]
            rows = q8[group * 4 : group * 4 + 4, j * BLOCK : (j + 1) * BLOCK]
            band = lax.dot_general(
                rows.reshape(4 * BLOCK, HDIM), keys, nt, preferred_element_type=jnp.float32
            )
            for hh in range(4):
                head = group * 4 + hh
                pieces = []
                for w in range(3):
                    code = code_ref[(step * GROUPS * 4 + head) * 4 + j + w]
                    other = triangle if w == 2 else jnp.zeros_like(triangle)
                    bias = jnp.where(
                        code == 0, tables[hh][:, w * BLOCK : (w + 1) * BLOCK], other
                    )
                    if w < 2:
                        bias = jnp.where(code == 2, NEG, bias)
                    pieces.append(bias)
                bscore = band[hh * BLOCK : (hh + 1) * BLOCK] + jnp.concatenate(pieces, axis=1)
                ck = cols[now, head, :, :HDIM]
                cv = cols[now, head, :, HDIM:]
                cscore = lax.dot_general(
                    rows[hh], ck, nt, preferred_element_type=jnp.float32
                ) + cbias_ref[pl.ds(head * 2 + j, 1), :]
                top = jnp.maximum(
                    jnp.max(bscore, axis=1, keepdims=True), jnp.max(cscore, axis=1, keepdims=True)
                )
                bw = jnp.exp2((bscore - top) * factor)
                cw = jnp.exp2((cscore - top) * factor)
                total = jnp.sum(bw, axis=1, keepdims=True) + jnp.sum(cw, axis=1, keepdims=True)
                mixed = jnp.dot(bw.astype(BF16), values, preferred_element_type=jnp.float32)
                mixed += jnp.dot(cw.astype(BF16), cv, preferred_element_type=jnp.float32)
                outs[head][j] = (mixed / total).astype(BF16)
    stacked = jnp.stack([jnp.concatenate(pair, axis=0) for pair in outs], axis=0)
    o_ref[...] = jnp.swapaxes(stacked, 0, 1)


def attend(slots, codes, queries, kv, halo, base, cbias, pairs):
    steps = KV_HEADS // GROUPS
    heads = GROUPS * 4
    tokens = queries.shape[0]
    return pl.pallas_call(
        attend_kernel,
        grid=(steps,),
        out_shape=jax.ShapeDtypeStruct(queries.shape, BF16),
        in_specs=[
            pl.BlockSpec(memory_space=pltpu.SMEM),
            pl.BlockSpec(memory_space=pltpu.SMEM),
            pl.BlockSpec((tokens, heads, HDIM), lambda i: (0, i, 0)),
            pl.BlockSpec((GROUPS, 256, 256), lambda i: (i, 0, 0)),
            pl.BlockSpec((GROUPS, 256, 256), lambda i: (i, 0, 0)),
            pl.BlockSpec((heads, 384), lambda i: (i, 0)),
            pl.BlockSpec((heads * 2, 512), lambda i: (i, 0)),
            pl.BlockSpec(memory_space=pl.ANY),
        ],
        out_specs=pl.BlockSpec((tokens, heads, HDIM), lambda i: (0, i, 0)),
        scratch_shapes=[
            pltpu.VMEM((2, heads, VSLOTS * BLOCK, 2 * HDIM), BF16),
            pltpu.SemaphoreType.DMA((2,)),
        ],
        compiler_params=pltpu.CompilerParams(vmem_limit_bytes=48 * 2**20),
    )(slots, codes, queries, kv, halo, base, cbias, pairs)


def body(queries, key_states, value_states, column_blocks, column_count, slash_offsets, slash_count):
    c = lax.axis_index("ctx")
    k = lax.axis_index("head")
    kv = jnp.swapaxes(jnp.concatenate([key_states, value_states], axis=2), 0, 1)

    block = column_blocks.reshape(HEADS * VSLOTS)
    index = jnp.arange(HEADS * VSLOTS, dtype=jnp.int32)
    live = (jnp.arange(VSLOTS, dtype=jnp.int32)[None] < column_count[:, None]).reshape(-1)
    group = index // (4 * VSLOTS)
    pid = block * KV_HEADS + group
    core = (block // 2) % 2
    device = block // 2
    first = live & ~jnp.any(
        (pid[:, None] == pid[None]) & live[None] & (index[None] < index[:, None]), axis=1
    )
    same_core = first[None] & (core[None] == core[:, None])
    rank = jnp.sum(same_core & (pid[None] < pid[:, None]), axis=1, dtype=jnp.int32)
    most = jnp.max(jnp.sum(same_core & live[:, None], axis=1, dtype=jnp.int32))
    load = jnp.max(
        jnp.sum(first[None] & live[:, None] & (device[None] == device[:, None]), axis=1, dtype=jnp.int32)
    )

    olive = jnp.arange(SSLOTS, dtype=jnp.int32)[None] < slash_count[:, None]
    spot = jnp.arange(3 * BLOCK, dtype=jnp.int32)
    seen = jnp.any(
        (2 * BLOCK - spot[None, :, None] == slash_offsets[:, None, :]) & olive[:, None, :], axis=2
    )
    base = jnp.where(seen, 0.0, NEG).astype(jnp.float32)
    q0 = (c * 2 + k) * 2
    near = q0 - 2 + jnp.arange(4, dtype=jnp.int32)
    live4 = live.reshape(HEADS, VSLOTS)
    listed = jnp.any((column_blocks[:, None, :] == near[None, :, None]) & live4[:, None, :], axis=2)
    codes = jnp.where(near[None] < 0, 2, listed.astype(jnp.int32)).reshape(-1)
    ahead = q0 + jnp.arange(2, dtype=jnp.int32) - 3
    cvis = live4[:, None, :] & (column_blocks[:, None, :] <= ahead[None, :, None])
    cbias = jnp.where(cvis, 0.0, NEG).astype(jnp.float32)
    cbias = jnp.broadcast_to(cbias.reshape(HEADS * 2, VSLOTS, 1), (HEADS * 2, VSLOTS, BLOCK))
    cbias = cbias.reshape(HEADS * 2, VSLOTS * BLOCK)

    def run(Q, R, collective_id):
        mine = first & (device == c * 2 + k)
        turn = jnp.arange(R * 8, dtype=jnp.int32)
        hit = mine[None] & (rank[None] % (8 * R) == turn[:, None])
        sel = jnp.sum(jnp.where(hit, group * 2 + block % 2, 0), axis=1, dtype=jnp.int32)
        wanted = jnp.arange(Q, dtype=jnp.int32) * 8 + c // 8
        hit = (first & (core == k))[None] & (rank[None] == wanted[:, None])
        own = jnp.sum(jnp.where(hit, block // 4, 0), axis=1, dtype=jnp.int32)
        slots = jnp.where(live, core * (Q * 8) + rank, 0)
        pairs, halo = gather_pairs(sel, own, kv.reshape(16, BLOCK, 256), Q, R, collective_id)
        return attend(
            slots, codes, queries, kv, halo.reshape(KV_HEADS, 256, 256), base, cbias,
            pairs.reshape(2 * Q * 8, BLOCK, 256),
        )

    small = (most <= 7 * 8) & (load <= 8)
    return lax.cond(small, lambda: run(7, 1, 0), lambda: run(16, 2, 1))


def solution(mesh):
    placed = (
        P(("ctx", "head"), None, None),
        P(("ctx", "head"), None, None),
        P(("ctx", "head"), None, None),
        P(),
        P(),
        P(),
        P(),
    )
    return jax.shard_map(
        body, mesh=mesh, in_specs=placed, out_specs=P(("ctx", "head"), None, None), check_vma=False
    )
```

time: 692 us -> 97.6 us (0.14)
  blocking collectives: 419 us -> 0 us
  matrix products: 118 us -> 0 us
  local copies, waits for them, and re-layouts: 102 us -> 8.74 us
  Pallas kernels: 0 us -> 82.6 us
  other arithmetic: 25 us -> 4.18 us
  starting transfers between devices: 18.4 us -> 0 us
    psum x1 -> x0, blocking collectives: 364 us -> none  [body(): columns = lax.psum(payload, 'ctx').astype(jnp.bfloat16)]
    dot_general x16 -> x0, matrix products: 118 us -> none  [the longest x4 80 us: body(): jnp.einsum('qhd,kd->hqk', query_rows, window_rows[:, :head_depth], prefer...]
    pallas_call x0 -> x2, Pallas kernels: none -> 82.6 us  [the longest x1 56.7 us: gather_pairs(): pl.pallas_call(functools.partial(gather_kernel, Q, R), out_shape=(jax.Sha...]
    gather x1 -> x0, local copies, waits for them, and re-layouts: 81.5 us -> none  [body(): picked = pairs_local[safe_rows, owner_head[:, None]]]
    all_to_all x1 -> x0, blocking collectives: 54.6 us -> none  [body(): lax.all_to_all(outputs, 'head', split_axis=0, concat_axis=1, tiled=True)]
    all_to_all x3 -> x0, starting transfers between devices: 14 us -> none  [the longest x1 4.9 us: body(): lax.all_to_all(key_states, 'head', split_axis=1, concat_axis=0, tiled=True)]
    reduce_sum x5 -> x4, other arithmetic: 11.1 us -> 0.61 us  [the longest x1 0.2 us: body(): jnp.sum(first[None] & live[:, None] & (device[None] == device[:, None]),...]
  transfers between devices with their start and end apart: 4 -> 0, of which waited for: 2 -> 0; matrix products, arithmetic and copies ran while one was open for 17% -> 0% of each run, Pallas kernels for 0% -> 0%
where the time goes in v1:
time: 97.6 us; the launch traced here: 97.3 us
  Pallas kernels  82.6 us (85%)
  local copies, waits for them, and re-layouts  8.74 us (9%)
  other arithmetic  4.18 us (4%)
  between operations  1.46 us (1%)
    pallas_call x1, Pallas kernels, gather_pairs(): pl.pallas_call(functools.partial(gather_kernel, Q, R), out_shape=(jax.Sha...  56.7 us
    pallas_call x1, Pallas kernels, attend(): pl.pallas_call(attend_kernel, grid=(steps,), out_shape=jax.ShapeDtypeStru...  25.8 us
    unnamed x13, local copies, waits for them, and re-layouts  4.47 us
    cond x3, local copies, waits for them, and re-layouts  2.97 us

profile of v1, /device:TPU:1, one launch (start us, length us, event | category | flops | bytes accessed | tf_op | source)
XLA Modules:
  0.0 97.3 jit_solution(16231372752868749329)
XLA Ops:
  0.0 0.7 iota_compare_fusion.3
  0.7 0.8 and_reduce_fusion
  1.5 0.1 copy.66
  1.6 0.1 lt.106
  1.7 0.8 copy.67
  2.4 0.1 reshape.317
  2.6 0.2 fusion.11
  2.8 0.2 convert_reduce_fusion
  3.0 0.6 reduce_max.18
  4.3 0.6 reduce_max.19
  5.6 0.1 and_convert_fusion
  5.7 0.0 copy-start.2
  5.7 0.0 copy-start.4
  5.7 0.0 copy-start.5
  5.7 0.0 copy-start.6
  5.7 1.3 %copy.68 = bf16[256,8,128]{2,0,1:T(8,128)(2,1)S(1)} copy(bf16[256,8,128]{2,1,0:T(8,128)(2,1)} %param.10) | data formatting | bytes 1048576 | tf_op args[1]
  7.0 1.1 %copy.69 = bf16[256,8,128]{2,0,1:T(8,128)(2,1)S(1)} copy(bf16[256,8,128]{2,1,0:T(8,128)(2,1)} %param.11) | data formatting | bytes 1048576 | tf_op args[2]
  8.1 0.1 maximum_bitcast_fusion
  8.2 0.0 copy-done.2
  8.2 0.0 copy-done.4
  8.2 0.0 copy-done.5
  8.3 0.0 copy-done.6
  8.3 87.7 %conditional.1 = (bf16[256,32,128]{2,1,0:T(8,128)(2,1)S(1)}) conditional(s32[]{:T(128)} %convert_element_type.19, (s32[128]{0:T(128)S(1)}, s32[128,128]{1,0:T(8,128)S(1)}, pred[128]{0:T(512)(128)(4,1)S(1)}, s32[]{:T(128)}, s32[]{:T(128)}, /*index=5*/s32[128]{0:T(128)S(1)}, pred[128]{0:T(512)(128)(4,1)S(1)}, s32[128]{0:T(128)S(1)}, ...), branch_computations={%region_8.11_spmd.clone, %region_11.14_spmd.clone} | conditional | flops 629785 | bytes 67679280 | solution.py:369
  8.3 0.1 reduce_sum.73
  8.5 0.2 select_reduce_fusion.2.own_ref
  8.7 0.1 select_reduce_fusion.3.sel_ref
  8.8 0.1 broadcast_compare_fusion.2
  8.9 0.1 le.59
  9.0 0.1 copy.75
  9.1 0.1 copy.64
  9.2 0.1 copy.74
  9.2 0.3 fusion.5
  9.5 0.1 copy.73
  9.6 0.1 select_n.158.code_ref
  9.8 0.1 and.304
  9.8 0.1 and.303
  10.0 0.1 copy.65
  10.1 0.1 broadcast_in_dim.137
  10.2 56.7 %branch_1_fun.2 = (bf16[2,7,4,4,4,16,256]{6,5,4,3,2,1,0:T(8,128)(2,1)S(1)}, bf16[16,128,256]{2,1,0:T(8,128)(2,1)S(1)}) custom-call(s32[8]{0:T(128)S(1)} %select_reduce_fusion.3.sel_ref, s32[7]{0:T(128)S(1)} %select_reduce_fusion.2.own_ref, bf16[16,128,256]{2,1,0:T(8,128)(2,1)S(1)} %bitcast.29), custom_call_target="tpu_custom_call" | custom-call | tf_op jit(solution)/shard_map/cond/branch_1_fun/pallas_call | solution.py:171
  67.0 0.0 copy-start.1
  67.0 3.0 %copy-done.1 = bf16[2,7,4,4,4,16,256]{6,5,4,3,2,1,0:T(8,128)(2,1)} copy-done((bf16[2,7,4,4,4,16,256]{6,5,4,3,2,1,0:T(8,128)(2,1)}, bf16[2,7,4,4,4,16,256]{6,5,4,3,2,1,0:T(8,128)(2,1)S(1)}, u32[]{:S(2)}) %copy-start.1) | copy-done | bytes 7340056 | tf_op jit(solution)/shard_map/cond
  69.9 25.8 %branch_1_fun.3 = bf16[256,32,128]{2,1,0:T(8,128)(2,1)S(1)} custom-call(s32[128]{0:T(128)S(1)} %get-tuple-element.531.slot_ref, s32[128]{0:T(128)S(1)} %select_n.158.code_ref, bf16[256,32,128]{2,1,0:T(8,128)(2,1)S(1)} %get-tuple-element.293.q_ref, bf16[8,256,256]{2,1,0:T(8,128)(2,1)S(1)} %get-tuple-element.281.kv_ref, bf16[8,256,256]{2,1,0:T(8,128)(2,1)S(1)} %bitcast.25, ...), custom_call_target="tpu_custom_call" | custom-call | tf_op jit(solution)/shard_map/cond/branch_1_fun/pallas_call | solution.py:291
  96.0 0.0 copy-start.3
  96.0 1.3 %copy-done.3 = bf16[256,32,128]{2,1,0:T(8,128)(2,1)} copy-done((bf16[256,32,128]{2,1,0:T(8,128)(2,1)}, bf16[256,32,128]{2,1,0:T(8,128)(2,1)S(1)}, u32[]{:S(2)}) %copy-start.3) | copy-done | bytes 2097176
  (19 shorter events, 0.1 us)
Async XLA Ops:
  5.7 2.6 %copy-start.2 = (bf16[256,32,128]{2,1,0:T(8,128)(2,1)S(1)}, bf16[256,32,128]{2,1,0:T(8,128)(2,1)}, u32[]{:S(2)}) copy-start(bf16[256,32,128]{2,1,0:T(8,128)(2,1)} %param.9) | copy-start | bytes 6291460
  5.7 2.6 %copy-start.4 = (s32[32,16]{0,1:T(8,128)S(1)}, s32[32,16]{0,1:T(8,128)}, u32[]{:S(2)}) copy-start(s32[32,16]{0,1:T(8,128)} %param.14) | copy-start | bytes 6148
  5.7 2.6 %copy-start.5 = (s32[32,4]{0,1:T(4,128)S(1)}, s32[32,4]{0,1:T(4,128)}, u32[]{:S(2)}) copy-start(s32[32,4]{0,1:T(4,128)} %param.12) | copy-start | bytes 1540
  5.7 2.5 %copy-start.6 = (s32[32]{0:T(128)S(1)}, s32[32]{0:T(128)}, u32[]{:S(2)}) copy-start(s32[32]{0:T(128)} %param.15) | copy-start | bytes 388
  67.0 3.0 %copy-start.1 = (bf16[2,7,4,4,4,16,256]{6,5,4,3,2,1,0:T(8,128)(2,1)}, bf16[2,7,4,4,4,16,256]{6,5,4,3,2,1,0:T(8,128)(2,1)S(1)}, u32[]{:S(2)}) copy-start(bf16[2,7,4,4,4,16,256]{6,5,4,3,2,1,0:T(8,128)(2,1)S(1)} %get-tuple-element.289) | copy-start | bytes 22020100 | tf_op jit(solution)/shard_map/cond
  96.0 1.3 %copy-start.3 = (bf16[256,32,128]{2,1,0:T(8,128)(2,1)}, bf16[256,32,128]{2,1,0:T(8,128)(2,1)S(1)}, u32[]{:S(2)}) copy-start(bf16[256,32,128]{2,1,0:T(8,128)(2,1)S(1)} %get-tuple-element.537) | copy-start | bytes 6291460

commit v2 on v0

v2 whole, which is shorter than its diff:
```python
import functools
import math

import jax
import jax.numpy as jnp
from jax import lax
from jax.experimental import pallas as pl
from jax.experimental.pallas import tpu as pltpu
from jax.sharding import PartitionSpec as P

HEADS = 32
KV_HEADS = 8
HDIM = 128
BLOCK = 128
VSLOTS = 4
SSLOTS = 16
BAND = 256
CTX = 64
SIDE = 4
NEG = -1e30
MESH = pl.DeviceIdType.MESH
BF16 = jnp.bfloat16
F32 = jnp.float32
FACTOR = 1.4426950408889634 / math.sqrt(HDIM)
NT = (((1,), (1,)), ((), ()))
SLOT, CODE, CSEE, SEL, OWN = 0, 128, 256, 512, 528
WORDS = 544


def kernel(
    Q, R, tab, base_ref, q_hbm, k_hbm, v_hbm, pk_hbm, pv_hbm, o_hbm,
    qv, kin, vin, pkin, pvin, kvt, halo, send, recv, home, g_all, tables, qt, acc, tops, outs,
    in_sem, out_sem, s1_send, s1_recv, a_send, a_recv, b_send, b_recv, sib_send, sib_recv,
):
    c = lax.axis_index("ctx")
    k = lax.axis_index("head")
    coords = (c // 16, (c // 4) % 4, c % 4)
    fetch = [
        pltpu.make_async_copy(k_hbm, kin, in_sem.at[0]),
        pltpu.make_async_copy(v_hbm, vin, in_sem.at[1]),
        pltpu.make_async_copy(q_hbm, qv, in_sem.at[2]),
        pltpu.make_async_copy(pk_hbm, pkin, in_sem.at[3]),
        pltpu.make_async_copy(pv_hbm, pvin, in_sem.at[4]),
    ]
    for copy in fetch:
        copy.start()
    barrier = pltpu.get_barrier_semaphore()

    @pl.loop(1, CTX)
    def _(d):
        pl.semaphore_signal(barrier, inc=1, device_id={"ctx": (c + d) % CTX}, device_id_type=MESH)

    pl.semaphore_signal(barrier, inc=1, device_id={"head": 1 - k}, device_id_type=MESH)

    fetch[0].wait()
    fetch[1].wait()
    kt = jnp.swapaxes(kin[...], 0, 1)
    vt = jnp.swapaxes(vin[...], 0, 1)
    kvt[:, :, :HDIM] = kt.reshape(16, BLOCK, HDIM)
    kvt[:, :, HDIM:] = vt.reshape(16, BLOCK, HDIM)
    for r in range(R):
        for u in range(8):
            send[r, u] = kvt[tab[SEL + r * 8 + u]]
    pl.semaphore_wait(barrier, CTX)

    @pl.loop(1, CTX)
    def _(d):
        p = (c + d) % CTX
        for r in range(R):
            pltpu.make_async_remote_copy(
                src_ref=send.at[r, p // 8, pl.ds((p % 8) * 16, 16)],
                dst_ref=recv.at[r, c],
                send_sem=s1_send,
                recv_sem=s1_recv,
                device_id={"ctx": p},
                device_id_type=MESH,
            ).start()

    for r in range(R):
        recv[r, c] = send[r, c // 8, pl.ds((c % 8) * 16, 16)]

    fetch[3].wait()
    fetch[4].wait()
    halo[:, :, :HDIM] = jnp.swapaxes(pkin[...], 0, 1).reshape(16, BLOCK, HDIM)
    halo[:, :, HDIM:] = jnp.swapaxes(pvin[...], 0, 1).reshape(16, BLOCK, HDIM)

    fetch[2].wait()

    for i in range(2):
        qt[i * 16 : i * 16 + 16] = jnp.swapaxes(qv[:, i * 16 : i * 16 + 16, :], 0, 1)

    @pl.loop(0, HEADS)
    def _(h):
        line = jnp.broadcast_to(base_ref[pl.ds(h, 1), :], (BLOCK, 3 * BLOCK))
        tables[h] = pltpu.roll(line, 0, 1, stride=1, stride_axis=0)

    row = lax.broadcasted_iota(jnp.int32, (BLOCK, BLOCK), 0)
    col = lax.broadcasted_iota(jnp.int32, (BLOCK, BLOCK), 1)
    triangle = jnp.where(col <= row, 0.0, NEG)
    ones = jnp.ones((3 * BLOCK, HDIM), BF16)

    def band(first, last):
        @pl.loop(first, last)
        def _(g):
            blocks = [halo[2 * g], halo[2 * g + 1], kvt[2 * g], kvt[2 * g + 1]]
            for j in range(2):
                window = jnp.concatenate(blocks[j : j + 3], axis=0)
                rows = qt[pl.ds(g * 4, 4), j * BLOCK : (j + 1) * BLOCK, :]
                score = lax.dot_general(
                    rows.reshape(4 * BLOCK, HDIM), window[:, :HDIM], NT, preferred_element_type=F32
                )
                weights = []
                for hh in range(4):
                    h = g * 4 + hh
                    pieces = []
                    for w in range(3):
                        code = tab[CODE + h * 4 + j + w]
                        cut = slice(w * BLOCK, (w + 1) * BLOCK)
                        plain = tables[h, :, cut]
                        if w == 2:
                            bias = jnp.where(code == 1, triangle, plain)
                        else:
                            least = jnp.where(code == 1, 0.0, NEG)
                            most = jnp.where(code == 2, NEG, 0.0)
                            bias = jnp.minimum(jnp.maximum(plain, least), most)
                        pieces.append(score[hh * BLOCK : (hh + 1) * BLOCK, cut] + bias)
                    masked = jnp.concatenate(pieces, axis=1)
                    top = jnp.max(masked, axis=1, keepdims=True)
                    weights.append(jnp.exp2((masked - top) * FACTOR).astype(BF16))
                    tops[h, pl.ds(j * BLOCK, BLOCK), :] = jnp.broadcast_to(top, (BLOCK, HDIM))
                both = jnp.concatenate([window[:, HDIM:], ones], axis=1)
                mixed = jnp.dot(
                    jnp.concatenate(weights, axis=0), both, preferred_element_type=F32
                )
                acc[pl.ds(g * 4, 4), j * BLOCK : (j + 1) * BLOCK, :] = mixed.reshape(
                    4, BLOCK, 2 * HDIM
                )

    others = recv.at[:, pl.ds(0, CTX - 1)]
    pltpu.make_async_copy(others, others, s1_recv).wait()
    for q in range(Q):
        home[q] = recv[q % R, tab[OWN + q]]

    bounds = [0, (Q + 2) // 3, (2 * Q + 2) // 3, Q]

    def view(t, index, half=None):
        low, high = bounds[t], bounds[t + 1]
        middle = (low + high + 1) // 2
        if half == 0:
            high = middle
        if half == 1:
            low = middle
        x, y, z = index
        yh, yl = (slice(None), slice(None)) if y is None else (y // 2, y % 2)
        x = slice(None) if x is None else x
        z = slice(None) if z is None else z
        return g_all.at[pl.ds(k * Q + low, high - low), x, yh, yl, z]

    def moved(axis, delta, axis2=0, delta2=0):
        there = list(coords)
        there[axis] = (there[axis] + delta) % SIDE
        there[axis2] = (there[axis2] + delta2) % SIDE
        return {"ctx": there[0] * 16 + there[1] * 4 + there[2]}

    for t in range(3):
        low, high = bounds[t], bounds[t + 1]
        pltpu.make_async_copy(home.at[low:high], view(t, coords), a_recv.at[t]).start()

    @pl.loop(1, 16)
    def _(d):
        for t in range(3):
            low, high = bounds[t], bounds[t + 1]
            pltpu.make_async_remote_copy(
                src_ref=home.at[low:high], dst_ref=view(t, coords),
                send_sem=a_send.at[t], recv_sem=a_recv.at[t],
                device_id=moved(t, d // 4, (t + 1) % 3, d % 4), device_id_type=MESH,
            ).start()

    band(0, 4)

    across = []

    def to_sibling(ref):
        i = len(across)
        copy = pltpu.make_async_remote_copy(
            src_ref=ref, dst_ref=ref, send_sem=sib_send.at[i], recv_sem=sib_recv.at[i],
            device_id={"head": 1 - k}, device_id_type=MESH,
        )
        copy.start()
        across.append(copy)

    def slab(t, pos, half=None):
        index = [None, None, None]
        index[(t + 2) % 3] = pos
        return view(t, index, half)

    def push(t, pos, half, i, delta):
        ref = slab(t, pos, half)
        copy = pltpu.make_async_remote_copy(
            src_ref=ref, dst_ref=ref, send_sem=b_send.at[t, i], recv_sem=b_recv.at[t, i],
            device_id=moved((t + 2) % 3, delta), device_id_type=MESH,
        )
        copy.start()
        return copy

    sent = []
    for t in range(3):
        me = coords[(t + 2) % 3]
        whole = slab(t, me)
        pltpu.make_async_copy(whole, whole, a_recv.at[t]).wait()
        sent.append(
            [
                push(t, me, 0, 0, 1),
                push(t, me, 1, 1, -1),
                push(t, me, 1, 2, 1),
                push(t, me, 0, 3, -1),
            ]
        )
    for t in range(3):
        to_sibling(slab(t, coords[(t + 2) % 3]))
    band(4, 6)
    for t in range(3):
        me = coords[(t + 2) % 3]
        left, right = (me + 3) % 4, (me + 1) % 4
        sent[t][0].wait_recv()
        sent[t].append(push(t, left, 0, 4, 1))
        sent[t][1].wait_recv()
        sent[t].append(push(t, right, 1, 5, -1))
        to_sibling(slab(t, left, 0))
        to_sibling(slab(t, right, 1))
    band(6, 8)
    for t in range(3):
        me = coords[(t + 2) % 3]
        left, right = (me + 3) % 4, (me + 1) % 4
        sent[t][2].wait_recv()
        to_sibling(slab(t, left, 1))
        sent[t][3].wait_recv()
        to_sibling(slab(t, right, 0))
    for t in range(3):
        opposite = (coords[(t + 2) % 3] + 2) % 4
        sent[t][4].wait_recv()
        to_sibling(slab(t, opposite, 0))
        sent[t][5].wait_recv()
        to_sibling(slab(t, opposite, 1))
    for copy in across:
        copy.wait_recv()

    ones4 = jnp.ones((VSLOTS * BLOCK, HDIM), BF16)

    def columns_of(first, last):
        @pl.loop(first, last, step=4)
        def _(base):
            heads = [base + i for i in range(4)]
            loaded, scores = [], []
            for h in heads:
                tiles = []
                for s in range(VSLOTS):
                    at = tab[SLOT + h * VSLOTS + s]
                    tile = g_all[at // 8, (at % 8) // 2, at % 2]
                    tiles.append(tile.reshape(BLOCK, 2 * HDIM))
                columns = jnp.concatenate(tiles, axis=0)
                loaded.append(columns)
                scores.append(
                    lax.dot_general(qt[h], columns[:, :HDIM], NT, preferred_element_type=F32)
                )
            ready = []
            for h, score in zip(heads, scores):
                parts = []
                for j in range(2):
                    pieces = []
                    for s in range(VSLOTS):
                        see = tab[CSEE + (h * 2 + j) * VSLOTS + s]
                        bias = jnp.where(see == 1, 0.0, NEG)
                        pieces.append(
                            score[j * BLOCK : (j + 1) * BLOCK, s * BLOCK : (s + 1) * BLOCK] + bias
                        )
                    parts.append(jnp.concatenate(pieces, axis=1))
                masked = jnp.concatenate(parts, axis=0)
                top = tops[h]
                new = jnp.maximum(top, jnp.max(masked, axis=1, keepdims=True))
                weights = jnp.exp2((masked - new[:, :1]) * FACTOR).astype(BF16)
                ready.append((weights, jnp.exp2((top - new) * FACTOR)))
            for h, columns, (weights, keep) in zip(heads, loaded, ready):
                both = jnp.concatenate([columns[:, HDIM:], ones4], axis=1)
                mixed = jnp.dot(weights, both, preferred_element_type=F32)
                upper = acc[h, :, :HDIM] * keep + mixed[:, :HDIM]
                lower = acc[h, :, HDIM:] * keep + mixed[:, HDIM:]
                qt[h] = (upper / lower).astype(BF16)

    for i in range(2):
        sixteen = slice(i * 16, i * 16 + 16)
        columns_of(i * 16, i * 16 + 16)
        outs[i] = jnp.swapaxes(qt[sixteen], 0, 1)
        pltpu.make_async_copy(outs.at[i], o_hbm.at[:, sixteen, :], out_sem.at[i]).start()
    for i in range(2):
        sixteen = slice(i * 16, i * 16 + 16)
        pltpu.make_async_copy(outs.at[i], o_hbm.at[:, sixteen, :], out_sem.at[i]).wait()
    for t in range(3):
        for copy in sent[t]:
            copy.wait_send()
    for copy in across:
        copy.wait_send()
    for t in range(3):
        low, high = bounds[t], bounds[t + 1]
        for d in range(15):
            pltpu.make_async_copy(home.at[low:high], home.at[low:high], a_send.at[t]).wait()
    pltpu.make_async_copy(others, others, s1_send).wait()


def attend(table, base, queries, keys, values, before_keys, before_values, Q, R, collective_id):
    dma = pltpu.SemaphoreType.DMA
    return pl.pallas_call(
        functools.partial(kernel, Q, R),
        out_shape=jax.ShapeDtypeStruct(queries.shape, BF16),
        in_specs=[
            pl.BlockSpec(memory_space=pltpu.SMEM),
            pl.BlockSpec(memory_space=pltpu.VMEM),
            pl.BlockSpec(memory_space=pl.ANY),
            pl.BlockSpec(memory_space=pl.ANY),
            pl.BlockSpec(memory_space=pl.ANY),
            pl.BlockSpec(memory_space=pl.ANY),
            pl.BlockSpec(memory_space=pl.ANY),
        ],
        out_specs=pl.BlockSpec(memory_space=pl.ANY),
        scratch_shapes=[
            pltpu.VMEM((256, HEADS, HDIM), BF16),
            pltpu.VMEM((256, KV_HEADS, HDIM), BF16),
            pltpu.VMEM((256, KV_HEADS, HDIM), BF16),
            pltpu.VMEM((256, KV_HEADS, HDIM), BF16),
            pltpu.VMEM((256, KV_HEADS, HDIM), BF16),
            pltpu.VMEM((16, BLOCK, 2 * HDIM), BF16),
            pltpu.VMEM((16, BLOCK, 2 * HDIM), BF16),
            pltpu.VMEM((R, 8, BLOCK, 2 * HDIM), BF16),
            pltpu.VMEM((R, CTX, 16, 2 * HDIM), BF16),
            pltpu.VMEM((Q, 16, 2 * HDIM), BF16),
            pltpu.VMEM((2 * Q, 4, 2, 2, 4, 16, 2 * HDIM), BF16),
            pltpu.VMEM((HEADS, BLOCK, 3 * BLOCK), F32),
            pltpu.VMEM((HEADS, 256, HDIM), BF16),
            pltpu.VMEM((HEADS, 256, 2 * HDIM), F32),
            pltpu.VMEM((HEADS, 256, HDIM), F32),
            pltpu.VMEM((2, 256, 16, HDIM), BF16),
            dma((5,)),
            dma((2,)),
            dma(()),
            dma(()),
            dma((3,)),
            dma((3,)),
            dma((3, 6)),
            dma((3, 6)),
            dma((21,)),
            dma((21,)),
        ],
        compiler_params=pltpu.CompilerParams(
            collective_id=collective_id, has_side_effects=True, vmem_limit_bytes=60 * 2**20
        ),
    )(table, base, queries, keys, values, before_keys, before_values)


def body(queries, key_states, value_states, column_blocks, column_count, slash_offsets, slash_count):
    c = lax.axis_index("ctx")
    k = lax.axis_index("head")

    route = [(i, i + 1) for i in range(2 * CTX - 1)]
    before_keys = lax.ppermute(key_states, ("ctx", "head"), route)
    before_values = lax.ppermute(value_states, ("ctx", "head"), route)

    block = column_blocks.reshape(HEADS * VSLOTS)
    index = jnp.arange(HEADS * VSLOTS, dtype=jnp.int32)
    live = (jnp.arange(VSLOTS, dtype=jnp.int32)[None] < column_count[:, None]).reshape(-1)
    group = index // (4 * VSLOTS)
    pid = block * KV_HEADS + group
    core = (block // 2) % 2
    device = block // 2
    first = live & ~jnp.any(
        (pid[:, None] == pid[None]) & live[None] & (index[None] < index[:, None]), axis=1
    )
    same_core = first[None] & (core[None] == core[:, None])
    rank = jnp.sum(same_core & (pid[None] < pid[:, None]), axis=1, dtype=jnp.int32)
    load = jnp.sum(first[None] & (device[None] == device[:, None]), axis=1, dtype=jnp.int32)
    fits = jnp.all(~live | ((rank < 6 * 8) & (load <= 8)))

    olive = jnp.arange(SSLOTS, dtype=jnp.int32)[None] < slash_count[:, None]
    spot = jnp.arange(3 * BLOCK, dtype=jnp.int32)
    seen = jnp.any(
        (2 * BLOCK - spot[None, :, None] == slash_offsets[:, None, :]) & olive[:, None, :], axis=2
    )
    base = jnp.where(seen, 0.0, NEG).astype(F32)
    q0 = (c * 2 + k) * 2
    near = q0 - 2 + jnp.arange(4, dtype=jnp.int32)
    live4 = live.reshape(HEADS, VSLOTS)
    listed = jnp.any((column_blocks[:, None, :] == near[None, :, None]) & live4[:, None, :], axis=2)
    codes = jnp.where(near[None] < 0, 2, listed.astype(jnp.int32)).reshape(-1)
    ahead = q0 + jnp.arange(2, dtype=jnp.int32) - 3
    csee = live4[:, None, :] & (column_blocks[:, None, :] <= ahead[None, :, None])
    csee = csee.astype(jnp.int32).reshape(-1)

    def run(Q, R, collective_id):
        mine = first & (device == c * 2 + k)
        turn = jnp.arange(R * 8, dtype=jnp.int32)
        hit = mine[None] & (rank[None] % (8 * R) == turn[:, None])
        sel = jnp.sum(jnp.where(hit, group * 2 + block % 2, 0), axis=1, dtype=jnp.int32)
        wanted = jnp.arange(Q, dtype=jnp.int32) * 8 + c // 8
        hit = (first & (core == k))[None] & (rank[None] == wanted[:, None])
        own = jnp.sum(jnp.where(hit, block // 4, 0), axis=1, dtype=jnp.int32)
        slots = jnp.where(live, core * (Q * 8) + rank, 0)
        pad = lambda a: jnp.pad(a, (0, 16 - a.shape[0]))
        table = jnp.concatenate([slots, codes, csee, pad(sel), pad(own)])
        return attend(table, base, queries, key_states, value_states, before_keys, before_values, Q, R, collective_id)

    return lax.cond(fits, lambda: run(6, 1, 0), lambda: run(16, 2, 1))


def solution(mesh):
    placed = (
        P(("ctx", "head"), None, None),
        P(("ctx", "head"), None, None),
        P(("ctx", "head"), None, None),
        P(),
        P(),
        P(),
        P(),
    )
    return jax.shard_map(
        body, mesh=mesh, in_specs=placed, out_specs=P(("ctx", "head"), None, None), check_vma=False
    )
```

time: 692 us -> 76.6 us (0.11)
  blocking collectives: 419 us -> 0 us
  matrix products: 118 us -> 0 us
  local copies, waits for them, and re-layouts: 102 us -> 4.93 us
  Pallas kernels: 0 us -> 53.3 us
  other arithmetic: 25 us -> 4.64 us
  starting transfers between devices: 18.4 us -> 6.85 us
    psum x1 -> x0, blocking collectives: 364 us -> none  [body(): columns = lax.psum(payload, 'ctx').astype(jnp.bfloat16)]
    dot_general x16 -> x0, matrix products: 118 us -> none  [the longest x4 80 us: body(): jnp.einsum('qhd,kd->hqk', query_rows, window_rows[:, :head_depth], prefer...]
    gather x1 -> x0, local copies, waits for them, and re-layouts: 81.5 us -> none  [body(): picked = pairs_local[safe_rows, owner_head[:, None]]]
    all_to_all x1 -> x0, blocking collectives: 54.6 us -> none  [body(): lax.all_to_all(outputs, 'head', split_axis=0, concat_axis=1, tiled=True)]
    pallas_call x0 -> x1, Pallas kernels: none -> 53.3 us  [attend(): pl.pallas_call(functools.partial(kernel, Q, R), out_shape=jax.ShapeDtypeS...]
    all_to_all x3 -> x0, starting transfers between devices: 14 us -> none  [the longest x1 4.9 us: body(): lax.all_to_all(key_states, 'head', split_axis=1, concat_axis=0, tiled=True)]
    reduce_sum x5 -> x3, other arithmetic: 11.1 us -> 0.5 us  [the longest x1 0.2 us: body(): jnp.sum(same_core & (pid[None] < pid[:, None]), axis=1, dtype=jnp.int32)]
  transfers between devices with their start and end apart: 4 -> 2, of which waited for: 2 -> 2; matrix products, arithmetic and copies ran while one was open for 17% -> 5% of each run, Pallas kernels for 0% -> 0%
where the time goes in v2:
time: 76.6 us; the launch traced here: 76.2 us
  Pallas kernels  53.3 us (70%)
  starting transfers between devices  6.85 us (9%)
  waiting for transfers between devices  5.79 us (8%)
  local copies, waits for them, and re-layouts  4.93 us (6%)
  other arithmetic  4.64 us (6%)
    pallas_call x1, Pallas kernels, attend(): pl.pallas_call(functools.partial(kernel, Q, R), out_shape=jax.ShapeDtypeS...  53.3 us
    ppermute x1, waiting for transfers between devices, body(): before_values = lax.ppermute(value_states, ('ctx', 'head'), route)  5.62 us
    ppermute x1, starting transfers between devices, body(): before_keys = lax.ppermute(key_states, ('ctx', 'head'), route)  4.93 us
    unnamed x2, local copies, waits for them, and re-layouts  2.09 us
    ppermute x1, starting transfers between devices, body(): before_values = lax.ppermute(value_states, ('ctx', 'head'), route)  1.92 us
    another operation x3, local copies, waits for them, and re-layouts  1.62 us
  transfers between devices with their start and end apart: 2, of which 2 were waited for; matrix products, arithmetic and copies ran while one was open for 5% of the time, Pallas kernels for 0%

profile of v2, /device:TPU:1, one launch (start us, length us, event | category | flops | bytes accessed | tf_op | source)
XLA Modules:
  0.0 76.2 jit_solution(214566374925551215)
XLA Ops:
  0.0 4.9 %collective-permute-start = (bf16[256,8,128]{2,1,0:T(8,128)(2,1)}, bf16[256,8,128]{2,1,0:T(8,128)(2,1)S(1)}, u32[]{:S(2)}, u32[]{:S(2)}) collective-permute-start(bf16[256,8,128]{2,1,0:T(8,128)(2,1)} %param.10), channel_id=1, source_target_pairs={{0,1},{1,2},{2,3},{3,4},{4,5},{5,6},{6,7},{7,8},{8,9},{9,10},{10,1... | collective-permute-start | bytes 1572872 | tf_op jit(solution)/shard_map/ppermute | solution.py:364
  4.9 1.9 %collective-permute-start.1 = (bf16[256,8,128]{2,1,0:T(8,128)(2,1)}, bf16[256,8,128]{2,1,0:T(8,128)(2,1)S(1)}, u32[]{:S(2)}, u32[]{:S(2)}) collective-permute-start(bf16[256,8,128]{2,1,0:T(8,128)(2,1)} %param.11), channel_id=1, source_target_pairs={{0,1},{1,2},{2,3},{3,4},{4,5},{5,6},{6,7},{7,8},{8,9},{9,10},{10,1... | collective-permute-start | bytes 1572872 | tf_op jit(solution)/shard_map/ppermute | solution.py:365
  6.9 0.7 iota_compare_fusion.3
  7.6 0.1 lt.113
  7.7 0.1 copy.45
  7.8 0.8 %copy.44 = s32[32,4]{1,0:T(8,128)S(1)} copy(s32[32,4]{0,1:T(4,128)} %param.12) | data formatting | bytes 1024 | tf_op args[3]
  8.6 0.8 %and_reduce_fusion = pred[32,4]{0,1:T(4,128)(4,1)S(1)} fusion(s32[32,4]{0,1:T(4,128)} %param.12, s32[4]{0:T(128)S(1)} %iota_add_fusion, pred[32,4]{0,1:T(4,128)(4,1)S(1)} %copy.45), kind=kLoop, calls=%fused_computation.64 | loop fusion | flops 1408 | bytes 784 | tf_op jit(solution)/shard_map/reduce_or | solution.py:391
  9.4 0.1 reshape.271
  9.5 0.2 fusion.11
  9.7 0.2 convert_reduce_fusion.1
  9.9 0.6 or_reduce_fusion
  11.2 0.2 collective-permute-done
  11.4 5.6 %collective-permute-done.1 = bf16[256,8,128]{2,1,0:T(8,128)(2,1)S(1)} collective-permute-done((bf16[256,8,128]{2,1,0:T(8,128)(2,1)}, bf16[256,8,128]{2,1,0:T(8,128)(2,1)S(1)}, u32[]{:S(2)}, u32[]{:S(2)}) %collective-permute-start.1) | collective-permute-done | bytes 524320 | tf_op jit(solution)/shard_map/ppermute | solution.py:365
  17.0 57.9 %conditional.1 = (bf16[256,32,128]{2,1,0:T(8,128)(2,1)S(1)}) conditional(s32[]{:T(128)} %convert_element_type.23, (s32[128]{0:T(128)S(1)}, s32[128]{0:T(128)S(1)}, pred[128]{0:T(512)(128)(4,1)S(1)}, s32[]{:T(128)}, s32[]{:T(128)}, /*index=5*/s32[128]{0:T(128)S(1)}, pred[128]{0:T(512)(128)(4,1)S(1)}, s32[128]{0:T(128)S(1)}, ...), branch_computations={%region_6.9_spmd.clone, %region_9.12_spmd.clone} | conditional | flops 613529 | bytes 108327 | solution.py:410
  17.1 0.2 select_reduce_fusion.2
  17.2 0.1 select_reduce_fusion.3
  17.4 0.7 broadcast_compare_fusion.2
  18.1 0.8 %copy.51 = s32[32,16]{1,0:T(8,128)S(1)} copy(s32[32,16]{0,1:T(8,128)} %get-tuple-element.423) | data formatting | bytes 4096 | tf_op jit(solution)/shard_map
  18.9 0.3 fusion.5
  19.2 0.8 %copy.50 = s32[32,4]{1,0:T(8,128)S(1)} copy(s32[32,4]{0,1:T(4,128)} %get-tuple-element.419) | data formatting | bytes 1024 | tf_op jit(solution)/shard_map
  19.9 0.1 fusion.6
  20.0 0.1 reshape.273
  20.1 0.1 copy.49
  20.2 0.1 select_n.146
  20.4 0.7 concatenate.7.tab
  21.0 0.6 broadcast_select_fusion.2.base_ref
  21.6 53.3 %branch_1_fun.1 = bf16[256,32,128]{2,1,0:T(8,128)(2,1)S(1)} custom-call(s32[544]{0:T(1024)} %concatenate.7.tab, f32[32,384]{1,0:T(8,128)} %broadcast_select_fusion.2.base_ref, bf16[256,32,128]{2,1,0:T(8,128)(2,1)} %get-tuple-element.280.q_hbm, bf16[256,8,128]{2,1,0:T(8,128)(2,1)} %get-tuple-element.274.k_hbm, bf16[256,8,128]{2,1,0:T(8,128)(2,1)} %get-tuple-element.275.v_hbm, ...), custom_call_target="tpu_custom_call" | custom-call | tf_op jit(solution)/shard_map/cond/branch_1_fun/pallas_call | solution.py:312
  74.9 1.3 %copy.55 = bf16[256,32,128]{2,1,0:T(8,128)(2,1)} copy(bf16[256,32,128]{2,1,0:T(8,128)(2,1)S(1)} %get-tuple-element.110) | data formatting | bytes 4194304
  (16 shorter events, 0.1 us)
Async XLA Ops:
  0.0 11.4 %collective-permute-start = (bf16[256,8,128]{2,1,0:T(8,128)(2,1)}, bf16[256,8,128]{2,1,0:T(8,128)(2,1)S(1)}, u32[]{:S(2)}, u32[]{:S(2)}) collective-permute-start(bf16[256,8,128]{2,1,0:T(8,128)(2,1)} %param.10), channel_id=1, source_target_pairs={{0,1},{1,2},{2,3},{3,4},{4,5},{5,6},{6,7},{7,8},{8,9},{9,10},{10,1... | collective-permute-start | bytes 1572872 | tf_op jit(solution)/shard_map/ppermute | solution.py:364
  4.9 12.0 %collective-permute-start.1 = (bf16[256,8,128]{2,1,0:T(8,128)(2,1)}, bf16[256,8,128]{2,1,0:T(8,128)(2,1)S(1)}, u32[]{:S(2)}, u32[]{:S(2)}) collective-permute-start(bf16[256,8,128]{2,1,0:T(8,128)(2,1)} %param.11), channel_id=1, source_target_pairs={{0,1},{1,2},{2,3},{3,4},{4,5},{5,6},{6,7},{7,8},{8,9},{9,10},{10,1... | collective-permute-start | bytes 1572872 | tf_op jit(solution)/shard_map/ppermute | solution.py:365

commit v3 on v2

--- a/solution.py
+++ b/solution.py
@@ -23,14 +23,15 @@
 F32 = jnp.float32
 FACTOR = 1.4426950408889634 / math.sqrt(HDIM)
 NT = (((1,), (1,)), ((), ()))
-SLOT, CODE, CSEE, SEL, OWN = 0, 128, 256, 512, 528
-WORDS = 544
+SLOT, CODE, CSEE, REST, FITS = 0, 2, 3, 5, 6
+SMALL = 6
 
 
 def kernel(
-    Q, R, tab, base_ref, q_hbm, k_hbm, v_hbm, pk_hbm, pv_hbm, o_hbm,
-    qv, kin, vin, pkin, pvin, kvt, halo, send, recv, home, g_all, tables, qt, acc, tops, outs,
+    Q, R, t_hbm, off_hbm, cnt_hbm, q_hbm, k_hbm, v_hbm, o_hbm,
+    tab, offsets, counts, qv, kin, vin, kvt, halo, send, recv, home, g_all, tables, qt, acc, tops, outs,
     in_sem, out_sem, s1_send, s1_recv, a_send, a_recv, b_send, b_recv, sib_send, sib_recv,
+    halo_send, halo_recv,
 ):
     c = lax.axis_index("ctx")
     k = lax.axis_index("head")
@@ -39,8 +40,9 @@
         pltpu.make_async_copy(k_hbm, kin, in_sem.at[0]),
         pltpu.make_async_copy(v_hbm, vin, in_sem.at[1]),
         pltpu.make_async_copy(q_hbm, qv, in_sem.at[2]),
-        pltpu.make_async_copy(pk_hbm, pkin, in_sem.at[3]),
-        pltpu.make_async_copy(pv_hbm, pvin, in_sem.at[4]),
+        pltpu.make_async_copy(t_hbm, tab, in_sem.at[3]),
+        pltpu.make_async_copy(off_hbm, offsets, in_sem.at[4]),
+        pltpu.make_async_copy(cnt_hbm, counts, in_sem.at[5]),
     ]
     for copy in fetch:
         copy.start()
@@ -51,6 +53,12 @@
         pl.semaphore_signal(barrier, inc=1, device_id={"ctx": (c + d) % CTX}, device_id_type=MESH)
 
     pl.semaphore_signal(barrier, inc=1, device_id={"head": 1 - k}, device_id_type=MESH)
+
+    @pl.when(k == 0)
+    def _():
+        pl.semaphore_signal(
+            barrier, inc=1, device_id={"ctx": (c + CTX - 1) % CTX, "head": 1}, device_id_type=MESH
+        )
 
     fetch[0].wait()
     fetch[1].wait()
@@ -58,10 +66,11 @@
     vt = jnp.swapaxes(vin[...], 0, 1)
     kvt[:, :, :HDIM] = kt.reshape(16, BLOCK, HDIM)
     kvt[:, :, HDIM:] = vt.reshape(16, BLOCK, HDIM)
+    fetch[3].wait()
     for r in range(R):
         for u in range(8):
-            send[r, u] = kvt[tab[SEL + r * 8 + u]]
-    pl.semaphore_wait(barrier, CTX)
+            send[r, u] = kvt[tab[REST, (0 if R == 1 else 16) + r * 8 + u]]
+    pl.semaphore_wait(barrier, CTX + k)
 
     @pl.loop(1, CTX)
     def _(d):
@@ -76,22 +85,39 @@
                 device_id_type=MESH,
             ).start()
 
+    tails = []
+
+    def pass_on(first, last):
+        for g in range(first, last):
+            copy = pltpu.make_async_remote_copy(
+                src_ref=kvt.at[2 * g : 2 * g + 2], dst_ref=halo.at[2 * g : 2 * g + 2],
+                send_sem=halo_send.at[g], recv_sem=halo_recv.at[g],
+                device_id={"ctx": (c + k) % CTX, "head": 1 - k}, device_id_type=MESH,
+            )
+            copy.start()
+            tails.append(copy)
+
+    pass_on(0, 3)
     for r in range(R):
         recv[r, c] = send[r, c // 8, pl.ds((c % 8) * 16, 16)]
 
-    fetch[3].wait()
-    fetch[4].wait()
-    halo[:, :, :HDIM] = jnp.swapaxes(pkin[...], 0, 1).reshape(16, BLOCK, HDIM)
-    halo[:, :, HDIM:] = jnp.swapaxes(pvin[...], 0, 1).reshape(16, BLOCK, HDIM)
-
     fetch[2].wait()
 
     for i in range(2):
         qt[i * 16 : i * 16 + 16] = jnp.swapaxes(qv[:, i * 16 : i * 16 + 16, :], 0, 1)
 
+    fetch[4].wait()
+    fetch[5].wait()
+    spot = 2 * BLOCK - lax.broadcasted_iota(jnp.int32, (1, 3 * BLOCK), 1)
+
     @pl.loop(0, HEADS)
     def _(h):
-        line = jnp.broadcast_to(base_ref[pl.ds(h, 1), :], (BLOCK, 3 * BLOCK))
+        used = counts[h]
+        line = jnp.full((1, 3 * BLOCK), NEG, F32)
+        for s in range(SSLOTS):
+            offset = jnp.where(s < used, offsets[s, h], -1000)
+            line = jnp.where(spot == offset, 0.0, line)
+        line = jnp.broadcast_to(line, (BLOCK, 3 * BLOCK))
         tables[h] = pltpu.roll(line, 0, 1, stride=1, stride_axis=0)
 
     row = lax.broadcasted_iota(jnp.int32, (BLOCK, BLOCK), 0)
@@ -100,6 +126,9 @@
     ones = jnp.ones((3 * BLOCK, HDIM), BF16)
 
     def band(first, last):
+        for g in range(first, last):
+            tails[g].wait_recv()
+
         @pl.loop(first, last)
         def _(g):
             blocks = [halo[2 * g], halo[2 * g + 1], kvt[2 * g], kvt[2 * g + 1]]
@@ -114,7 +143,7 @@
                     h = g * 4 + hh
                     pieces = []
                     for w in range(3):
-                        code = tab[CODE + h * 4 + j + w]
+                        code = tab[CODE, h * 4 + j + w]
                         cut = slice(w * BLOCK, (w + 1) * BLOCK)
                         plain = tables[h, :, cut]
                         if w == 2:
@@ -139,7 +168,7 @@
     others = recv.at[:, pl.ds(0, CTX - 1)]
     pltpu.make_async_copy(others, others, s1_recv).wait()
     for q in range(Q):
-        home[q] = recv[q % R, tab[OWN + q]]
+        home[q] = recv[q % R, tab[REST, (32 if R == 1 else 48) + q]]
 
     bounds = [0, (Q + 2) // 3, (2 * Q + 2) // 3, Q]
 
@@ -166,17 +195,19 @@
         low, high = bounds[t], bounds[t + 1]
         pltpu.make_async_copy(home.at[low:high], view(t, coords), a_recv.at[t]).start()
 
-    @pl.loop(1, 16)
-    def _(d):
-        for t in range(3):
-            low, high = bounds[t], bounds[t + 1]
+    for t in range(3):
+        low, high = bounds[t], bounds[t + 1]
+
+        @pl.loop(1, 16)
+        def _(d):
             pltpu.make_async_remote_copy(
                 src_ref=home.at[low:high], dst_ref=view(t, coords),
                 send_sem=a_send.at[t], recv_sem=a_recv.at[t],
                 device_id=moved(t, d // 4, (t + 1) % 3, d % 4), device_id_type=MESH,
             ).start()
 
-    band(0, 4)
+    pass_on(3, 7)
+    band(0, 2)
 
     across = []
 
@@ -218,7 +249,8 @@
         )
     for t in range(3):
         to_sibling(slab(t, coords[(t + 2) % 3]))
-    band(4, 6)
+    pass_on(7, 8)
+    band(2, 3)
     for t in range(3):
         me = coords[(t + 2) % 3]
         left, right = (me + 3) % 4, (me + 1) % 4
@@ -228,7 +260,7 @@
         sent[t].append(push(t, right, 1, 5, -1))
         to_sibling(slab(t, left, 0))
         to_sibling(slab(t, right, 1))
-    band(6, 8)
+    band(3, 6)
     for t in range(3):
         me = coords[(t + 2) % 3]
         left, right = (me + 3) % 4, (me + 1) % 4
@@ -242,34 +274,31 @@
         to_sibling(slab(t, opposite, 0))
         sent[t][5].wait_recv()
         to_sibling(slab(t, opposite, 1))
+    band(6, 8)
     for copy in across:
         copy.wait_recv()
 
     ones4 = jnp.ones((VSLOTS * BLOCK, HDIM), BF16)
 
     def columns_of(first, last):
-        @pl.loop(first, last, step=4)
+        @pl.loop(first, last, step=8)
         def _(base):
-            heads = [base + i for i in range(4)]
-            loaded, scores = [], []
-            for h in heads:
+            def scored(h):
                 tiles = []
                 for s in range(VSLOTS):
-                    at = tab[SLOT + h * VSLOTS + s]
+                    at = tab[SLOT + (R > 1), h * VSLOTS + s]
                     tile = g_all[at // 8, (at % 8) // 2, at % 2]
                     tiles.append(tile.reshape(BLOCK, 2 * HDIM))
                 columns = jnp.concatenate(tiles, axis=0)
-                loaded.append(columns)
-                scores.append(
-                    lax.dot_general(qt[h], columns[:, :HDIM], NT, preferred_element_type=F32)
-                )
-            ready = []
-            for h, score in zip(heads, scores):
+                score = lax.dot_general(qt[h], columns[:, :HDIM], NT, preferred_element_type=F32)
+                return columns, score
+
+            def weighted(h, score):
                 parts = []
                 for j in range(2):
                     pieces = []
                     for s in range(VSLOTS):
-                        see = tab[CSEE + (h * 2 + j) * VSLOTS + s]
+                        see = tab[CSEE + j, h * VSLOTS + s]
                         bias = jnp.where(see == 1, 0.0, NEG)
                         pieces.append(
                             score[j * BLOCK : (j + 1) * BLOCK, s * BLOCK : (s + 1) * BLOCK] + bias
@@ -279,13 +308,22 @@
                 top = tops[h]
                 new = jnp.maximum(top, jnp.max(masked, axis=1, keepdims=True))
                 weights = jnp.exp2((masked - new[:, :1]) * FACTOR).astype(BF16)
-                ready.append((weights, jnp.exp2((top - new) * FACTOR)))
-            for h, columns, (weights, keep) in zip(heads, loaded, ready):
+                return weights, jnp.exp2((top - new) * FACTOR)
+
+            def finished(h, columns, weights, keep):
                 both = jnp.concatenate([columns[:, HDIM:], ones4], axis=1)
                 mixed = jnp.dot(weights, both, preferred_element_type=F32)
                 upper = acc[h, :, :HDIM] * keep + mixed[:, :HDIM]
                 lower = acc[h, :, HDIM:] * keep + mixed[:, HDIM:]
                 qt[h] = (upper / lower).astype(BF16)
+
+            ahead = scored(base)
+            for i in range(8):
+                h = base + i
+                columns, score = ahead
+                if i < 7:
+                    ahead = scored(h + 1)
+                finished(h, columns, *weighted(h, score))
 
     for i in range(2):
         sixteen = slice(i * 16, i * 16 + 16)
@@ -304,17 +342,18 @@
         low, high = bounds[t], bounds[t + 1]
         for d in range(15):
             pltpu.make_async_copy(home.at[low:high], home.at[low:high], a_send.at[t]).wait()
+    for copy in tails:
+        copy.wait_send()
     pltpu.make_async_copy(others, others, s1_send).wait()
 
 
-def attend(table, base, queries, keys, values, before_keys, before_values, Q, R, collective_id):
+def attend(table, offsets, counts, queries, keys, values, Q, R, collective_id):
     dma = pltpu.SemaphoreType.DMA
     return pl.pallas_call(
         functools.partial(kernel, Q, R),
         out_shape=jax.ShapeDtypeStruct(queries.shape, BF16),
         in_specs=[
-            pl.BlockSpec(memory_space=pltpu.SMEM),
-            pl.BlockSpec(memory_space=pltpu.VMEM),
+            pl.BlockSpec(memory_space=pl.ANY),
             pl.BlockSpec(memory_space=pl.ANY),
             pl.BlockSpec(memory_space=pl.ANY),
             pl.BlockSpec(memory_space=pl.ANY),
@@ -323,9 +362,10 @@
         ],
         out_specs=pl.BlockSpec(memory_space=pl.ANY),
         scratch_shapes=[
+            pltpu.SMEM((8, 128), jnp.int32),
+            pltpu.SMEM((SSLOTS, HEADS), jnp.int32),
+            pltpu.SMEM((HEADS,), jnp.int32),
             pltpu.VMEM((256, HEADS, HDIM), BF16),
-            pltpu.VMEM((256, KV_HEADS, HDIM), BF16),
-            pltpu.VMEM((256, KV_HEADS, HDIM), BF16),
             pltpu.VMEM((256, KV_HEADS, HDIM), BF16),
             pltpu.VMEM((256, KV_HEADS, HDIM), BF16),
             pltpu.VMEM((16, BLOCK, 2 * HDIM), BF16),
@@ -339,7 +379,7 @@
             pltpu.VMEM((HEADS, 256, 2 * HDIM), F32),
             pltpu.VMEM((HEADS, 256, HDIM), F32),
             pltpu.VMEM((2, 256, 16, HDIM), BF16),
-            dma((5,)),
+            dma((6,)),
             dma((2,)),
             dma(()),
             dma(()),
@@ -349,65 +389,108 @@
             dma((3, 6)),
             dma((21,)),
             dma((21,)),
+            dma((8,)),
+            dma((8,)),
         ],
         compiler_params=pltpu.CompilerParams(
             collective_id=collective_id, has_side_effects=True, vmem_limit_bytes=60 * 2**20
         ),
-    )(table, base, queries, keys, values, before_keys, before_values)
-
-
-def body(queries, key_states, value_states, column_blocks, column_count, slash_offsets, slash_count):
+    )(table, offsets, counts, queries, keys, values)
+
+
+def table_kernel(blocks_hbm, counts_hbm, o_ref, blocks, counts, column, sems):
+    copies = [
+        pltpu.make_async_copy(blocks_hbm, blocks, sems.at[0]),
+        pltpu.make_async_copy(counts_hbm, counts, sems.at[1]),
+    ]
+    for copy in copies:
+        copy.start()
     c = lax.axis_index("ctx")
     k = lax.axis_index("head")
-
-    route = [(i, i + 1) for i in range(2 * CTX - 1)]
-    before_keys = lax.ppermute(key_states, ("ctx", "head"), route)
-    before_values = lax.ppermute(value_states, ("ctx", "head"), route)
-
-    block = column_blocks.reshape(HEADS * VSLOTS)
-    index = jnp.arange(HEADS * VSLOTS, dtype=jnp.int32)
-    live = (jnp.arange(VSLOTS, dtype=jnp.int32)[None] < column_count[:, None]).reshape(-1)
-    group = index // (4 * VSLOTS)
-    pid = block * KV_HEADS + group
-    core = (block // 2) % 2
-    device = block // 2
-    first = live & ~jnp.any(
-        (pid[:, None] == pid[None]) & live[None] & (index[None] < index[:, None]), axis=1
+    for copy in copies:
+        copy.wait()
+    for i in range(HEADS * VSLOTS):
+        block = blocks[i % VSLOTS, i // VSLOTS]
+        block = jnp.where(i % VSLOTS < counts[i // VSLOTS], block, block + 1024)
+        column[pl.ds(i, 1), :] = jnp.full((1, 128), block, jnp.int32)
+    shape = (128, 128)
+    down, across = column[...], column[...].astype(F32).T.astype(jnp.int32)
+    i, j = lax.broadcasted_iota(jnp.int32, shape, 0), lax.broadcasted_iota(jnp.int32, shape, 1)
+    live_i, live_j = down < 1024, across < 1024
+    pid_i = down * KV_HEADS + i // 16
+    pid_j = across * KV_HEADS + j // 16
+    core_i, core_j = (down // 2) % 2, (across // 2) % 2
+    same = pid_i == pid_j
+
+    def total(mask, axis):
+        return jnp.sum(jnp.where(mask, 1.0, 0.0), axis=axis, keepdims=True).astype(jnp.int32)
+
+    def wide(a):
+        return jnp.broadcast_to(a, shape)
+
+    first_i = live_i & (wide(total(same & live_j & (j < i), 1)) == 0)
+    first_j = live_j & (wide(total(same & live_i & (i < j), 0)) == 0)
+    rank_i = wide(total(first_j & (core_i == core_j) & (pid_j < pid_i), 1))
+    rank_j = wide(total(first_i & (core_i == core_j) & (pid_i < pid_j), 0))
+    load_i = wide(total(first_j & (down // 2 == across // 2), 1))
+    bad = total(live_i & ((rank_i >= SMALL * 8) | (load_i > 8)), 0)
+    q0 = (c * 2 + k) * 2
+    near = q0 - 2 + j % 4
+    listed = total(live_i & (i // 4 == j // 4) & (down == near), 0)
+    codes = jnp.where(near[:1] < 0, 2, jnp.minimum(listed, 1))
+    mine = first_i & (down // 2 == c * 2 + k)
+    kept = first_i & (core_i == k) & (rank_i == (j % 16) * 8 + c // 8)
+    hit = jnp.where(
+        j < 16,
+        jnp.where(mine & (rank_i % 8 == j), 1, 0),
+        jnp.where(
+            j < 32, jnp.where(mine & (rank_i % 16 == j - 16), 1, 0), jnp.where(kept, 1, 0)
+        ),
     )
-    same_core = first[None] & (core[None] == core[:, None])
-    rank = jnp.sum(same_core & (pid[None] < pid[:, None]), axis=1, dtype=jnp.int32)
-    load = jnp.sum(first[None] & (device[None] == device[:, None]), axis=1, dtype=jnp.int32)
-    fits = jnp.all(~live | ((rank < 6 * 8) & (load <= 8)))
-
-    olive = jnp.arange(SSLOTS, dtype=jnp.int32)[None] < slash_count[:, None]
-    spot = jnp.arange(3 * BLOCK, dtype=jnp.int32)
-    seen = jnp.any(
-        (2 * BLOCK - spot[None, :, None] == slash_offsets[:, None, :]) & olive[:, None, :], axis=2
-    )
-    base = jnp.where(seen, 0.0, NEG).astype(F32)
-    q0 = (c * 2 + k) * 2
-    near = q0 - 2 + jnp.arange(4, dtype=jnp.int32)
-    live4 = live.reshape(HEADS, VSLOTS)
-    listed = jnp.any((column_blocks[:, None, :] == near[None, :, None]) & live4[:, None, :], axis=2)
-    codes = jnp.where(near[None] < 0, 2, listed.astype(jnp.int32)).reshape(-1)
-    ahead = q0 + jnp.arange(2, dtype=jnp.int32) - 3
-    csee = live4[:, None, :] & (column_blocks[:, None, :] <= ahead[None, :, None])
-    csee = csee.astype(jnp.int32).reshape(-1)
+    value = jnp.where(j < 32, (i // 16) * 2 + down % 2, down // 4)
+    rest = jnp.sum(jnp.where(hit == 1, value, 0).astype(F32), axis=0, keepdims=True)
+
+    def seen(ahead):
+        return jnp.where(across[:1] <= ahead, 1, 0)
+
+    for row, q in ((0, SMALL), (1, 16)):
+        place = core_j[:1] * (q * 8) + rank_j[:1]
+        o_ref[row : row + 1, :] = jnp.where(across[:1] < 1024, place, 0)
+    o_ref[CODE : CODE + 1, :] = codes
+    o_ref[CSEE : CSEE + 1, :] = seen(q0 - 3)
+    o_ref[CSEE + 1 : CSEE + 2, :] = seen(q0 - 2)
+    o_ref[REST : REST + 1, :] = rest.astype(jnp.int32)
+    o_ref[FITS : FITS + 1, :] = jnp.where(bad == 0, 1, 0)
+    o_ref[FITS + 1 : FITS + 2, :] = jnp.zeros((1, 128), jnp.int32)
+
+
+def tables_of(column_blocks, column_count):
+    return pl.pallas_call(
+        table_kernel,
+        out_shape=jax.ShapeDtypeStruct((8, 128), jnp.int32),
+        in_specs=[pl.BlockSpec(memory_space=pl.ANY), pl.BlockSpec(memory_space=pl.ANY)],
+        out_specs=pl.BlockSpec(memory_space=pltpu.VMEM),
+        scratch_shapes=[
+            pltpu.SMEM((VSLOTS, HEADS), jnp.int32),
+            pltpu.SMEM((HEADS,), jnp.int32),
+            pltpu.VMEM((128, 128), jnp.int32),
+            pltpu.SemaphoreType.DMA((2,)),
+        ],
+        cost_estimate=pl.CostEstimate(flops=10**6, bytes_accessed=10**5, transcendentals=0),
+    )(column_blocks, column_count)
+
+
+def body(queries, key_states, value_states, column_blocks, column_count, slash_offsets, slash_count):
+    table = tables_of(column_blocks.T, column_count)
+    offsets = slash_offsets.T
 
     def run(Q, R, collective_id):
-        mine = first & (device == c * 2 + k)
-        turn = jnp.arange(R * 8, dtype=jnp.int32)
-        hit = mine[None] & (rank[None] % (8 * R) == turn[:, None])
-        sel = jnp.sum(jnp.where(hit, group * 2 + block % 2, 0), axis=1, dtype=jnp.int32)
-        wanted = jnp.arange(Q, dtype=jnp.int32) * 8 + c // 8
-        hit = (first & (core == k))[None] & (rank[None] == wanted[:, None])
-        own = jnp.sum(jnp.where(hit, block // 4, 0), axis=1, dtype=jnp.int32)
-        slots = jnp.where(live, core * (Q * 8) + rank, 0)
-        pad = lambda a: jnp.pad(a, (0, 16 - a.shape[0]))
-        table = jnp.concatenate([slots, codes, csee, pad(sel), pad(own)])
-        return attend(table, base, queries, key_states, value_states, before_keys, before_values, Q, R, collective_id)
-
-    return lax.cond(fits, lambda: run(6, 1, 0), lambda: run(16, 2, 1))
+        return attend(
+            table, offsets, slash_count, queries, key_states, value_states,
+            Q, R, collective_id,
+        )
+
+    return lax.cond(table[FITS, 0] == 1, lambda: run(SMALL, 1, 0), lambda: run(16, 2, 1))
 
 
 def solution(mesh):

time: 76.6 us -> 60.4 us (0.79)
  starting transfers between devices: 6.85 us -> 0 us
  waiting for transfers between devices: 5.79 us -> 0 us
  other arithmetic: 4.64 us -> 0 us
  Pallas kernels: 53.3 us -> 56.6 us
  local copies, waits for them, and re-layouts: 4.93 us -> 1.84 us
    ppermute x2 -> x0, starting transfers between devices: 6.85 us -> none  [the longest x1 4.93 us: body(): before_keys = lax.ppermute(key_states, ('ctx', 'head'), route)]
    ppermute x2 -> x0, waiting for transfers between devices: 5.79 us -> none  [the longest x1 5.62 us: body(): before_values = lax.ppermute(value_states, ('ctx', 'head'), route)]
    pallas_call x1, Pallas kernels: 53.3 us -> 55.3 us  [attend(): pl.pallas_call(functools.partial(kernel, Q, R), out_shape=jax.ShapeDtypeS...]
    another operation x3 -> x0, local copies, waits for them, and re-layouts: 1.62 us -> none
    lt x3 -> x0, other arithmetic: 1.47 us -> none  [the longest x1 0.73 us: body(): olive = jnp.arange(SSLOTS, dtype=jnp.int32)[None] < slash_count[:, None]]
    pallas_call x0 -> x1, Pallas kernels: none -> 1.26 us  [tables_of(): pl.pallas_call(table_kernel, out_shape=jax.ShapeDtypeStruct((8, 128), jnp...]
    reduce_or x3 -> x0, other arithmetic: 1.24 us -> none  [the longest x1 0.77 us: body(): jnp.any((column_blocks[:, None, :] == near[None, :, None]) & live4[:, Non...]
    unnamed x2 -> x1, local copies, waits for them, and re-layouts: 2.09 us -> 1.32 us
  transfers between devices with their start and end apart: 2 -> 0, of which waited for: 2 -> 0; matrix products, arithmetic and copies ran while one was open for 5% -> 0% of each run, Pallas kernels for 0% -> 0%
where the time goes in v3:
time: 60.4 us; the launch traced here: 59.3 us
  Pallas kernels  56.6 us (94%)
  local copies, waits for them, and re-layouts  1.84 us (3%)
  between operations  0.67 us (1%)
    pallas_call x1, Pallas kernels, attend(): pl.pallas_call(functools.partial(kernel, Q, R), out_shape=jax.ShapeDtypeS...  55.3 us
    unnamed x1, local copies, waits for them, and re-layouts  1.32 us
    pallas_call x1, Pallas kernels, tables_of(): pl.pallas_call(table_kernel, out_shape=jax.ShapeDtypeStruct((8, 128), jnp...  1.26 us

profile of v3, /device:TPU:1, one launch (start us, length us, event | category | flops | bytes accessed | tf_op | source)
XLA Modules:
  0.0 59.3 jit_solution(7323089698773256730)
XLA Ops:
  0.0 1.3 %shard_map.83 = s32[8,128]{1,0:T(8,128)S(1)} custom-call(s32[4,32]{1,0:T(4,128)} %bitcast.5, s32[32]{0:T(128)} %counts_hbm.1), custom_call_target="tpu_custom_call" | custom-call | flops 1000000 | bytes 100000 | tf_op jit(solution)/shard_map/pallas_call | solution.py:468
  1.3 0.5 slice.3
  2.4 55.6 %conditional.1 = (bf16[256,32,128]{2,1,0:T(8,128)(2,1)S(1)}) conditional(s32[]{:T(128)} %bitcast.1, (s32[8,128]{1,0:T(8,128)S(1)}, s32[16,32]{1,0:T(8,128)}, s32[32]{0:T(128)}, bf16[256,32,128]{2,1,0:T(8,128)(2,1)}, bf16[256,8,128]{2,1,0:T(8,128)(2,1)}, /*index=5*/bf16[256,8,128]{2,1,0:T(8,128)(2,1)}) %tuple.16, (s32[8,128]{1,0:T(8,128)S(1)}, ...), branch_computations={%region_0.0_spmd, %region_1.0_spmd} | conditional | bytes 8 | solution.py:493
  2.5 55.3 %branch_1_fun.1 = bf16[256,32,128]{2,1,0:T(8,128)(2,1)S(1)} custom-call(s32[8,128]{1,0:T(8,128)S(1)} %get-tuple-element.38.t_hbm, s32[16,32]{1,0:T(8,128)} %get-tuple-element.39.off_hbm, s32[32]{0:T(128)} %get-tuple-element.54.cnt_hbm, bf16[256,32,128]{2,1,0:T(8,128)(2,1)} %get-tuple-element.56.q_hbm, bf16[256,8,128]{2,1,0:T(8,128)(2,1)} %get-tuple-element.58.k_hbm, ...), custom_call_target="tpu_custom_call" | custom-call | tf_op jit(solution)/shard_map/cond/branch_1_fun/pallas_call | solution.py:352
  58.0 1.3 %copy.21 = bf16[256,32,128]{2,1,0:T(8,128)(2,1)} copy(bf16[256,32,128]{2,1,0:T(8,128)(2,1)S(1)} %get-tuple-element.44) | data formatting | bytes 4194304
